TPU v7x, 128 devices: a whole 4x4x4 slice. The times are simulated.
128 devices in a mesh: rep: 4 (over y_lo, core), fsdp: 32 (over z, x, y_hi).
Axes of the slice: x: 4, y: 4 (y_hi: 2, y_lo: 2; y = y_hi * 2 + y_lo), z: 4, core: 2. Of those that a mesh axis runs over, the one named last changes fastest.
Arguments:
- acts: bfloat16 [98304, 8192], P(('rep', 'fsdp')), may hold values from -24 to 24
- cots: bfloat16 [98304, 1024], P(('rep', 'fsdp')), may hold values from -0.038085938 to 0.038085938
- inner_w: float32 [4, 8192, 1024], P('rep', 'fsdp'), may hold values from -6 to 6
- first_moment: float32 [4, 8192, 1024], P('rep', 'fsdp'), may hold values from -6 to 6
- second_moment: float32 [4, 8192, 1024], P('rep', 'fsdp'), may hold values from 0.05 to 2
- anchor: float32 [8192, 1024], P('fsdp'), may hold values from -6 to 6
- momentum: float32 [8192, 1024], P('fsdp'), may hold values from -3 to 3
- fragment: int32 [1], replicated, may hold values from 0 to 7
Outputs:
- new_w: float32 [4, 8192, 1024], P('rep', 'fsdp')
- new_first: float32 [4, 8192, 1024], P('rep', 'fsdp')
- new_second: float32 [4, 8192, 1024], P('rep', 'fsdp')
- new_anchor: float32 [8192, 1024], P('fsdp')
- new_momentum: float32 [8192, 1024], P('fsdp')
Inputs may be any that keep to these rules, and one draw needn't show every extreme that they name: fragment k selects head k of the key projection for k < 4, else head k - 4 of the value projection.
All inputs are finite; a program needn't handle non-finite values.
Results may differ from a plain program's by a relative error of at most 0.0003.
Values may be sent and summed in bfloat16 or wider, within the bound.
No kernel may reach another device: no remote copies, remote signals or barrier semaphores. Data moves between devices by JAX's collectives and lax.ppermute only.
A program may use at most 192 MiB of HBM per device.

v0:
```python
import functools

import jax
import jax.numpy as jnp
from jax import lax
from jax.experimental import pallas as pl
from jax.experimental.pallas import tpu as pltpu
from jax.sharding import PartitionSpec as P

HEAD_DIM = 128
INNER_STEP = 100

beta_first = 0.9
beta_second = 0.95
epsilon = 1e-08
inner_rate = 0.00015
decay_rate = 0.1
outer_rate = 0.7
outer_factor = 0.9
mixing_share = 0.5

SENT = jnp.float16
WIDE, NARROW = 384, 256
RING = 4
TOK, ROWS = 768, 8192
BLOCK = 512
VMEM = 16 << 20


SHORT = pl.CostEstimate(flops=1, bytes_accessed=1, transcendentals=0)


def wide(value):
    return value.astype(jnp.float32)


def tie(value, *others):
    return lax.optimization_barrier((value, *others))[0]


def in_hbm(value):
    return pltpu.with_memory_space_constraint(value, pltpu.HBM)


SMEM_SPEC = pl.BlockSpec(memory_space=pltpu.SMEM)
VMEM_SPEC = pl.BlockSpec(memory_space=pltpu.VMEM)
ANY_SPEC = pl.BlockSpec(memory_space=pl.ANY)


def turned(left, right):
    return lax.dot_general(
        left, right, (((0,), (0,)), ((), ())), preferred_element_type=jnp.float32
    )


SLOTS = 3
PAIR = 2 * BLOCK


def streamed(acts, ids, held, sems, count):
    def copies(i):
        made = []
        for k in range(2):
            start = ids[2 * i + k] * BLOCK
            start = start if isinstance(start, int) else pl.multiple_of(start, BLOCK)
            source = acts.at[:, pl.ds(start, BLOCK)]
            target = held.at[i % SLOTS, :, k * BLOCK : (k + 1) * BLOCK]
            made.append(pltpu.make_async_copy(source, target, sems.at[i % SLOTS, k]))
        return made

    for i in range(min(SLOTS, count)):
        for copy in copies(i):
            copy.start()
    for i in range(count):
        for copy in copies(i):
            copy.wait()
        yield i, held.at[i % SLOTS]
        if i + SLOTS < count:
            for copy in copies(i + SLOTS):
                copy.start()


def rest_kernel(ids, acts, cots, *refs):
    relays, owns = refs[:4], refs[4:6]
    held, cots_here, own_here, sems, cots_sems, back_sems = refs[6:]
    copies = []
    for part in range(2):
        cut = slice(part * WIDE, (part + 1) * WIDE)
        copies.append(
            pltpu.make_async_copy(cots.at[:, cut], cots_here.at[:, cut], cots_sems.at[part])
        )
        copies[-1].start()
    back = []
    for i, left in streamed(acts, ids, held, sems, 8):
        part, k = i // 4, i % 4
        if k == 0:
            copies[part].wait()
        value = turned(left[...], cots_here[:, part * WIDE : (part + 1) * WIDE])
        if k < 2:
            relays[2 * part + k][...] = value
        else:
            slot, rows = 2 * part + k - 2, slice((k - 2) * PAIR, (k - 1) * PAIR)
            own_here[slot] = value
            copy = pltpu.make_async_copy(
                own_here.at[slot], owns[part].at[rows], back_sems.at[slot]
            )
            copy.start()
            back.append(copy)
    for copy in back:
        copy.wait()


def dot_rest(ids, acts, cots):
    return pl.pallas_call(
        rest_kernel,
        in_specs=[SMEM_SPEC, ANY_SPEC, ANY_SPEC],
        out_specs=[VMEM_SPEC] * 4 + [ANY_SPEC] * 2,
        out_shape=[pltpu.VMEM((PAIR, WIDE), jnp.float32)] * 4
        + [pltpu.HBM((2 * PAIR, WIDE), jnp.float32)] * 2,
        scratch_shapes=[
            pltpu.VMEM((SLOTS, TOK, PAIR), acts.dtype),
            pltpu.VMEM((TOK, 2 * WIDE), cots.dtype),
            pltpu.VMEM((4, PAIR, WIDE), jnp.float32),
            pltpu.SemaphoreType.DMA((SLOTS, 2)),
            pltpu.SemaphoreType.DMA((2,)),
            pltpu.SemaphoreType.DMA((4,)),
        ],
        compiler_params=pltpu.CompilerParams(vmem_limit_bytes=16 << 20),
        cost_estimate=SHORT,
        name="dot_rest",
    )(ids, in_hbm(acts), in_hbm(cots))


def first_kernel(ids, acts, cots, *refs):
    firsts, (mine, other) = refs[:4], refs[4:6]
    held, cots_here, mine_here, sems, cots_sems, back_sems = refs[6:]
    own = ids[24]
    copies = []
    for k, cut in enumerate((slice(0, WIDE), slice(2 * WIDE, 1024), slice(WIDE, 2 * WIDE))):
        copies.append(pltpu.make_async_copy(cots.at[:, cut], cots_here.at[:, cut], cots_sems.at[k]))
        copies[-1].start()
    back = []
    for i, left in streamed(acts, ids, held, sems, 12):
        if i == 0:
            for copy in copies:
                copy.wait()
        if i < 4 or i >= 8:
            part, k = (0, i) if i < 4 else (1, i - 8)
            right = cots_here[:, part * WIDE : (part + 1) * WIDE]
            row = k % 2 * PAIR
            firsts[2 * part + k // 2][row : row + PAIR] = turned(left[...], right)
        if i < 8:
            for k in range(2):
                rows = pl.ds(pl.multiple_of(ids[2 * i + k] * 256, 256), 256)
                for to, side in ((mine_here, own), (other, 1 - own)):
                    half = left[:, pl.ds(pl.multiple_of(k * BLOCK + side * 256, 256), 256)]
                    to[rows] = turned(half, cots_here[:, 2 * WIDE :])
                copy = pltpu.make_async_copy(
                    mine_here.at[rows], mine.at[rows], back_sems.at[2 * i + k]
                )
                copy.start()
                back.append(copy)
    for copy in back:
        copy.wait()


def dot_first(ids, acts, cots):
    half = (ROWS // 2, NARROW)
    return pl.pallas_call(
        first_kernel,
        in_specs=[SMEM_SPEC, ANY_SPEC, ANY_SPEC],
        out_specs=[VMEM_SPEC] * 4 + [ANY_SPEC, VMEM_SPEC],
        out_shape=[pltpu.VMEM((2 * PAIR, WIDE), jnp.float32)] * 4
        + [pltpu.HBM(half, jnp.float32), pltpu.VMEM(half, jnp.float32)],
        scratch_shapes=[
            pltpu.VMEM((SLOTS, TOK, PAIR), acts.dtype),
            pltpu.VMEM(cots.shape, cots.dtype),
            pltpu.VMEM(half, jnp.float32),
            pltpu.SemaphoreType.DMA((SLOTS, 2)),
            pltpu.SemaphoreType.DMA((3,)),
            pltpu.SemaphoreType.DMA((16,)),
        ],
        compiler_params=pltpu.CompilerParams(vmem_limit_bytes=14 << 20),
        cost_estimate=SHORT,
        name="dot_first",
    )(ids, in_hbm(acts), in_hbm(cots))


AXES = ("rep", "fsdp")


def pairs_of(dz=0, dx=0, dh=0, dl=0, dc=0):
    place = lambda z, x, h, l, c: ((l * 2 + c) * RING + z) * RING * 2 + x * 2 + h
    return [
        (
            place(z, x, h, l, c),
            place((z + dz) % RING, (x + dx) % RING, (h + dh) % 2, (l + dl) % 2, (c + dc) % 2),
        )
        for z in range(RING)
        for x in range(RING)
        for h in range(2)
        for l in range(2)
        for c in range(2)
    ]


CHANNELS = {
    "z+": dict(dz=1),
    "z-": dict(dz=-1),
    "x+": dict(dx=1),
    "x-": dict(dx=-1),
    "z2": dict(dz=2),
    "x2": dict(dx=2),
    "y": dict(dh=1),
    "l": dict(dl=1),
    "c": dict(dc=1),
}


class Order:
    def __init__(self):
        self.arrived = {}
        self.last = None

    def after(self, value, *others):
        return value if self.last is None else tie(value, self.last, *others)

    def ran(self, value):
        self.last = value
        return value

    def send(self, value, step, channel=None):
        channel = channel or step
        if channel in self.arrived:
            value = tie(value, self.arrived[channel])
        got = lax.ppermute(value, AXES, pairs_of(**CHANNELS[step]))
        self.arrived[channel] = got
        return got


def outer_kernel(fragment, anchor, momentum, drift, new_anchor, new_momentum, mix):
    outer = drift[...]
    for k in range(anchor.shape[1] // HEAD_DIM):
        cut = slice(k * HEAD_DIM, (k + 1) * HEAD_DIM)
        chosen = fragment[0] == k
        momentum_part = outer_factor * momentum[:, cut] + outer
        anchor_next = anchor[:, cut] - outer_rate * (outer + outer_factor * momentum_part)
        new_momentum[:, cut] = jnp.where(chosen, momentum_part, momentum[:, cut])
        new_anchor[:, cut] = jnp.where(chosen, anchor_next, anchor[:, cut])

        @pl.when(chosen)
        def _():
            mix[...] = (1.0 - mixing_share) * anchor_next


def outer_step(fragment, anchor, momentum, drift):
    rows, cols = anchor.shape
    step = 64
    full = pl.BlockSpec((step, cols), lambda i, fragment: (i, 0))
    head = pl.BlockSpec((step, HEAD_DIM), lambda i, fragment: (i, 0))
    return pl.pallas_call(
        outer_kernel,
        grid_spec=pltpu.PrefetchScalarGridSpec(
            num_scalar_prefetch=1,
            grid=(rows // step,),
            in_specs=[full, full, head],
            out_specs=[full, full, head],
        ),
        out_shape=[
            jax.ShapeDtypeStruct(anchor.shape, jnp.float32),
            jax.ShapeDtypeStruct(anchor.shape, jnp.float32),
            jax.ShapeDtypeStruct((rows, HEAD_DIM), jnp.float32),
        ],
        compiler_params=pltpu.CompilerParams(vmem_limit_bytes=VMEM),
        cost_estimate=SHORT,
        name="outer_step",
    )(fragment, anchor, momentum, drift)


def inner_kernel(fragment, grad_a, grad_b, grad_c, weights, first, second, mix, *outs):
    new_w, new_first, new_second = outs
    for k in range(weights.shape[1] // HEAD_DIM):
        cut = slice(k * HEAD_DIM, (k + 1) * HEAD_DIM)
        part = (grad_a, grad_b, grad_c)[k // 3]
        grad = part[:, k % 3 * HEAD_DIM : (k % 3 + 1) * HEAD_DIM]
        moment = beta_first * first[:, cut] + (1.0 - beta_first) * grad
        square = beta_second * second[:, cut] + (1.0 - beta_second) * grad * grad
        new_first[:, cut] = moment
        new_second[:, cut] = square
        update = (
            moment
            / (1.0 - beta_first**INNER_STEP)
            / (jnp.sqrt(square / (1.0 - beta_second**INNER_STEP)) + epsilon)
        )
        stepped = weights[:, cut] - inner_rate * (update + decay_rate * weights[:, cut])
        mixed = mixing_share * stepped + mix[...]
        new_w[:, cut] = jnp.where(fragment[0] == k, mixed, stepped)


def inner_step(fragment, grad_a, grad_b, grad_c, weights, first, second, mix):
    rows, cols = weights.shape
    step = 64
    block = lambda width: pl.BlockSpec((step, width), lambda i, fragment: (i, 0))
    full, head = block(cols), block(HEAD_DIM)
    return pl.pallas_call(
        inner_kernel,
        grid_spec=pltpu.PrefetchScalarGridSpec(
            num_scalar_prefetch=1,
            grid=(rows // step,),
            in_specs=[block(WIDE), block(WIDE), block(NARROW), full, full, full, head],
            out_specs=[full] * 3,
        ),
        out_shape=[jax.ShapeDtypeStruct(weights.shape, jnp.float32)] * 3,
        compiler_params=pltpu.CompilerParams(vmem_limit_bytes=VMEM),
        cost_estimate=SHORT,
        name="inner_step",
    )(fragment, grad_a, grad_b, grad_c, weights, first, second, mix)


def low(value):
    return value[: value.shape[0] // 2]


def high(value):
    return value[value.shape[0] // 2 :]


def stack(upper, lower):
    return jnp.concatenate([upper, lower], 0)


def per_device(acts, cots, inner_w, first_moment, second_moment, anchor, momentum, fragment):
    span = HEAD_DIM
    me = lax.axis_index("fsdp").astype(jnp.int32)
    z, x, h = me >> 3, (me >> 1) & 3, me & 1
    order = Order()

    def blocks(part, quarters):
        ids = []
        for offset, half in quarters:
            for k in (2 * half, 2 * half + 1):
                if part == 0:
                    ids.append((((z + offset) & 3) << 2) + k)
                else:
                    ids.append((k << 2) + ((x + offset) & 3))
        return ids

    axes = ((0, "z"), (1, "x"))
    first, second, relayed = {}, {}, {}
    ids = blocks(0, [(2, 0), (1, 1), (-1, 0), (2, 1)])
    ids += blocks(0, [(0, 0), (0, 1), (1, 0), (-1, 1)])
    ids += blocks(1, [(2, 0), (1, 1), (-1, 0), (2, 1)])
    *terms, mine_c, other_c = dot_first(jnp.stack(ids + [h]), acts, cots)
    for term, channel in zip(terms, ("z+", "z-", "x+", "x-")):
        term = order.ran(order.after(term).astype(SENT))
        first[channel] = order.send(term, channel)

    weights = inner_w[0]
    column = fragment[0] * span
    groups = lax.axis_size("rep")
    cut = lambda v: lax.dynamic_slice_in_dim(v, column, span, 1)
    drift = order.after(cut(anchor) - cut(weights))
    drift = drift + order.send(drift, "c", "rep")

    other_c = order.ran(order.after(other_c, drift).astype(SENT))
    got_c = order.send(other_c, "y")

    ids = []
    for part, axis in axes:
        ids += blocks(part, [(1, 0), (-1, 1), (0, 0), (0, 1)])
    *terms, own_a, own_b = dot_rest(order.after(jnp.stack(ids)), acts, cots)
    order.ran(terms[0])
    relayed.update(zip(("z+", "z-", "x+", "x-"), terms))
    own = own_a, own_b

    def near(part):
        axis = axes[part][1]
        halves = []
        for half, way in ((low, "-"), (high, "+")):
            value = order.after(half(own[part])) + wide(half(first[axis + way]))
            halves.append(order.ran(value))
        return halves

    nears = []
    for part, axis in axes:
        term = order.after(relayed[axis + "+"]) + wide(low(first[axis + "+"]))
        second[axis + "+"] = order.send(order.ran(term.astype(SENT)), axis + "+")
        term = order.after(relayed[axis + "-"]) + wide(high(first[axis + "-"]))
        second[axis + "-"] = order.send(order.ran(term.astype(SENT)), axis + "-")
        if part == 0:
            nears.append(near(part))

    def at(array, position, axis=0):
        return lax.dynamic_index_in_dim(array, position & 3, axis, keepdims=False)

    def swap(array, axis, *others):
        other = lax.dynamic_index_in_dim(array, 1 - h, axis, keepdims=False)
        mine = lax.dynamic_index_in_dim(array, h, axis, keepdims=False)
        other = order.ran(order.after(other.astype(SENT), *others))
        return wide(mine) + wide(order.send(other, "y"))

    def ring_first(term, axis):
        up = order.ran(order.after(stack(low(term(2)), high(term(1)))))
        down = order.ran(order.after(stack(low(term(-1)), high(term(2)))))
        return order.send(up, axis + "+"), order.send(down, axis + "-")

    def ring_second(term, axis, first, *others):
        up, down = first
        value = (wide(low(term(1))) + wide(tie(low(up), *others))).astype(SENT)
        last_up = order.send(value, axis + "+")
        value = (wide(high(term(-1))) + wide(high(down))).astype(SENT)
        last_down = order.send(value, axis + "-")
        near, last = stack(low(down), high(up)), stack(last_up, last_down)
        return wide(term(0)) + wide(near) + wide(last)

    def direct_sum(term, axis, *others):
        up = order.send(term(1), axis + "+")
        far = order.send(tie(term(2), *others), axis + "2")
        down = order.send(tie(term(-1), *others), axis + "-")
        return (wide(term(0)) + wide(far)) + (wide(up) + wide(down))

    def total(part, halves):
        axis, sums = axes[part][1], []
        for half, way in zip(halves, "+-"):
            value = order.after(half) + wide(second[axis + way])
            sums.append(order.ran(value.astype(SENT)))
        return stack(*sums)

    sum_a = total(0, nears[0]).reshape(RING, BLOCK, WIDE)
    term_a = lambda k, s=sum_a: at(s, x + k)
    first_a = ring_first(term_a, "x")
    nears.append(near(1))
    drift = drift + order.send(tie(drift, got_c), "l", "rep")
    sum_c = (wide(got_c) + order.after(mine_c)).astype(SENT)
    sum_c = order.ran(sum_c).reshape(RING, 1024, NARROW)
    term_c = lambda k, s=sum_c: at(s, z + k)
    first_c = ring_first(term_c, "z")
    sum_b = total(1, nears[1]).reshape(RING, 2, 256, WIDE)
    sum_b = swap(sum_b, 1, drift).astype(SENT)
    sum_c = ring_second(term_c, "z", first_c).astype(SENT).reshape(RING, 256, NARROW)
    sum_a = ring_second(term_a, "x", first_a).reshape(2, 256, WIDE)
    drift = tie(drift, sum_b) / groups
    new_anchor, new_momentum, mix = outer_step(fragment, anchor, momentum, drift)

    grad_a = swap(sum_a, 0)
    grad_b = direct_sum(lambda k: at(sum_b, z + k), "z")
    grad_c = direct_sum(lambda k, s=sum_c: at(s, x + k), "x", grad_a)
    new_w, new_first, new_second = inner_step(
        fragment, grad_a, grad_b, grad_c,
        weights, first_moment[0], second_moment[0], mix,
    )
    return (new_w[None], new_first[None], new_second[None], new_anchor, new_momentum)


def solution(mesh):
    placed = (
        P(("rep", "fsdp"), None),
        P(("rep", "fsdp"), None),
        P("rep", "fsdp", None),
        P("rep", "fsdp", None),
        P("rep", "fsdp", None),
        P("fsdp", None),
        P("fsdp", None),
        P(),
    )
    return jax.shard_map(
        per_device,
        mesh=mesh,
        in_specs=placed,
        out_specs=(
            P("rep", "fsdp", None),
            P("rep", "fsdp", None),
            P("rep", "fsdp", None),
            P("fsdp", None),
            P("fsdp", None),
        ),
        check_vma=False,
    )
```

profile of v0, /device:TPU:0, one launch (start us, length us, event | category | flops | bytes accessed | tf_op | source)
XLA Modules:
  0.0 137.7 jit_solution(16184897807722776797)
XLA Ops:
  0.8 16.1 %dot_first.1 = (f32[2048,384]{1,0:T(8,128)S(1)}, f32[2048,384]{1,0:T(8,128)S(1)}, f32[2048,384]{1,0:T(8,128)S(1)}, f32[2048,384]{1,0:T(8,128)S(1)}, f32[4096,256]{1,0:T(8,128)}, /*index=5*/f32[4096,256]{1,0:T(8,128)S(1)}) custom-call(s32[25]{0:T(128)S(1)} %stack.147.ids, bf16[768,8192]{1,0:T(8,128)(2,1)} %acts.3, bf16[768,1024]{1,0:T(8,128)(2,1)} %cots.3), custom_call_target="tpu_custom_call" | custom-call | flops 1 | bytes 1 | tf_op jit(solution)/shard_map/dot_first/pallas_call | solution.py:169
  16.9 1.6 %convert_element_type.226 = f16[2048,384]{1,0:T(8,128)(2,1)} convert(f32[2048,384]{1,0:T(8,128)S(1)} %get-tuple-element.74) | non-fusion elementwise | flops 786432 | bytes 4718592 | tf_op jit(solution)/shard_map/convert_element_type | solution.py:355
  18.4 0.9 copy-done
  19.3 2.0 %collective-permute-start.1 = (f16[2048,384]{1,0:T(8,128)(2,1)}, f16[2048,384]{1,0:T(8,128)(2,1)}, u32[]{:S(2)}, u32[]{:S(2)}) collective-permute-start(f16[2048,384]{1,0:T(8,128)(2,1)} %convert_element_type.226), channel_id=1, source_target_pairs={{0,8},{32,40},{64,72},{96,104},{1,9},{33,41},{65,73},{97,105},{2,1... | collective-permute-start | bytes 4718600 | tf_op jit(solution)/shard_map/ppermute | solution.py:236
  21.3 1.4 %convert_element_type.227 = f16[2048,384]{1,0:T(8,128)(2,1)} convert(f32[2048,384]{1,0:T(8,128)S(1)} %get-tuple-element.75) | non-fusion elementwise | flops 786432 | bytes 4718592 | tf_op jit(solution)/shard_map/convert_element_type | solution.py:355
  22.8 2.1 %collective-permute-start.2 = (f16[2048,384]{1,0:T(8,128)(2,1)}, f16[2048,384]{1,0:T(8,128)(2,1)}, u32[]{:S(2)}, u32[]{:S(2)}) collective-permute-start(f16[2048,384]{1,0:T(8,128)(2,1)} %convert_element_type.227), channel_id=1, source_target_pairs={{0,24},{32,56},{64,88},{96,120},{1,25},{33,57},{65,89},{97,121},{2... | collective-permute-start | bytes 4718600 | tf_op jit(solution)/shard_map/ppermute | solution.py:236
  24.9 1.4 %convert_element_type.228 = f16[2048,384]{1,0:T(8,128)(2,1)} convert(f32[2048,384]{1,0:T(8,128)S(1)} %get-tuple-element.76) | non-fusion elementwise | flops 786432 | bytes 4718592 | tf_op jit(solution)/shard_map/convert_element_type | solution.py:355
  26.3 1.4 %convert_element_type.229 = f16[2048,384]{1,0:T(8,128)(2,1)} convert(f32[2048,384]{1,0:T(8,128)S(1)} %get-tuple-element.77) | non-fusion elementwise | flops 786432 | bytes 4718592 | tf_op jit(solution)/shard_map/convert_element_type | solution.py:355
  28.5 1.7 %collective-permute-start.3 = (f16[2048,384]{1,0:T(8,128)(2,1)}, f16[2048,384]{1,0:T(8,128)(2,1)}, u32[]{:S(2)}, u32[]{:S(2)}) collective-permute-start(f16[2048,384]{1,0:T(8,128)(2,1)} %convert_element_type.228), channel_id=1, source_target_pairs={{0,2},{32,34},{64,66},{96,98},{1,3},{33,35},{65,67},{97,99},{2,4},... | collective-permute-start | bytes 4718600 | tf_op jit(solution)/shard_map/ppermute | solution.py:236
  30.3 1.7 %collective-permute-start.4 = (f16[2048,384]{1,0:T(8,128)(2,1)}, f16[2048,384]{1,0:T(8,128)(2,1)}, u32[]{:S(2)}, u32[]{:S(2)}) collective-permute-start(f16[2048,384]{1,0:T(8,128)(2,1)} %convert_element_type.229), channel_id=1, source_target_pairs={{0,6},{32,38},{64,70},{96,102},{1,7},{33,39},{65,71},{97,103},{2,0... | collective-permute-start | bytes 4718600 | tf_op jit(solution)/shard_map/ppermute | solution.py:236
  32.1 2.5 %convert_element_type.230 = f16[4096,256]{1,0:T(8,128)(2,1)S(1)} convert(f32[4096,256]{1,0:T(8,128)} %copy-done) | non-fusion elementwise | flops 1048576 | bytes 6291456 | tf_op jit(solution)/shard_map/convert_element_type | solution.py:365
  34.6 3.2 %collective-permute-start.13 = (f16[4096,256]{1,0:T(8,128)(2,1)S(1)}, f16[4096,256]{1,0:T(8,128)(2,1)S(1)}, u32[]{:S(2)}, u32[]{:S(2)}) collective-permute-start(f16[4096,256]{1,0:T(8,128)(2,1)S(1)} %convert_element_type.230), channel_id=1, source_target_pairs={{0,1},{32,33},{64,65},{96,97},{1,0},{33,32},{65,64},{97,96},{2,3},... | collective-permute-start | bytes 6291464 | tf_op jit(solution)/shard_map/ppermute | solution.py:236
  37.8 12.0 %dot_rest.1 = (f32[1024,384]{1,0:T(8,128)S(1)}, f32[1024,384]{1,0:T(8,128)S(1)}, f32[1024,384]{1,0:T(8,128)S(1)}, f32[1024,384]{1,0:T(8,128)S(1)}, f32[2048,384]{1,0:T(8,128)}, /*index=5*/f32[2048,384]{1,0:T(8,128)}) custom-call(s32[16]{0:T(128)S(1)} %stack.129.ids, bf16[768,8192]{1,0:T(8,128)(2,1)} %acts.3, bf16[768,1024]{1,0:T(8,128)(2,1)} %cots.3), custom_call_target="tpu_custom_call" | custom-call | flops 1 | bytes 1 | tf_op jit(solution)/shard_map/dot_rest/pallas_call | solution.py:114
  49.8 2.2 %fusion.10 = (f32[1024,384]{1,0:T(8,128)S(1)}, f32[1024,384]{1,0:T(8,128)S(1)}) fusion(f32[2048,384]{1,0:T(8,128)} %get-tuple-element.81), kind=kLoop, calls=%fused_computation.69 | loop fusion | bytes 6291456 | tf_op jit(solution)/shard_map/slice | solution.py:321
  52.8 5.3 %collective-permute-done.1 = f16[2048,384]{1,0:T(8,128)(2,1)} collective-permute-done((f16[2048,384]{1,0:T(8,128)(2,1)}, f16[2048,384]{1,0:T(8,128)(2,1)}, u32[]{:S(2)}, u32[]{:S(2)}) %collective-permute-start.1) | collective-permute-done | bytes 1572896 | tf_op jit(solution)/shard_map/ppermute | solution.py:236
  58.2 1.4 %add_convert_fusion.8 = f16[1024,384]{1,0:T(8,128)(2,1)S(1)} fusion(f32[1024,384]{1,0:T(8,128)S(1)} %get-tuple-element.83, f16[2048,384]{1,0:T(8,128)(2,1)} %collective-permute-done.1), kind=kLoop, calls=%fused_computation.16 | loop fusion | flops 1179648 | bytes 3145728 | tf_op jit(solution)/shard_map/convert_element_type | solution.py:387
  59.6 1.4 %add_convert_fusion.7 = f16[1024,384]{1,0:T(8,128)(2,1)S(1)} fusion(f32[1024,384]{1,0:T(8,128)S(1)} %get-tuple-element.84, f16[2048,384]{1,0:T(8,128)(2,1)} %collective-permute-done.2), kind=kLoop, calls=%fused_computation.15 | loop fusion | flops 1179648 | bytes 3145728 | tf_op jit(solution)/shard_map/convert_element_type | solution.py:389
  61.0 3.0 %collective-permute-start.6 = (f16[1024,384]{1,0:T(8,128)(2,1)S(1)}, f16[1024,384]{1,0:T(8,128)(2,1)S(1)}, u32[]{:S(2)}, u32[]{:S(2)}) collective-permute-start(f16[1024,384]{1,0:T(8,128)(2,1)S(1)} %add_convert_fusion.7), channel_id=1, source_target_pairs={{0,24},{32,56},{64,88},{96,120},{1,25},{33,57},{65,89},{97,121},{2... | collective-permute-start | bytes 2359304 | tf_op jit(solution)/shard_map/ppermute | solution.py:236
  64.0 1.4 convert_add_fusion.4
  65.4 1.4 convert_add_fusion.3
  66.9 1.3 add_convert_fusion.6
  68.2 1.4 %add_convert_fusion.5 = f16[1024,384]{1,0:T(8,128)(2,1)S(1)} fusion(f32[1024,384]{1,0:T(8,128)S(1)} %get-tuple-element.90, f16[2048,384]{1,0:T(8,128)(2,1)} %collective-permute-done.4), kind=kLoop, calls=%fused_computation.11 | loop fusion | flops 1179648 | bytes 3145728 | tf_op jit(solution)/shard_map/convert_element_type | solution.py:389
  69.6 1.5 %collective-permute-start.9 = (f16[1024,384]{1,0:T(8,128)(2,1)S(1)}, f16[1024,384]{1,0:T(8,128)(2,1)S(1)}, u32[]{:S(2)}, u32[]{:S(2)}) collective-permute-start(f16[1024,384]{1,0:T(8,128)(2,1)S(1)} %add_convert_fusion.6), channel_id=1, source_target_pairs={{0,2},{32,34},{64,66},{96,98},{1,3},{33,35},{65,67},{97,99},{2,4},... | collective-permute-start | bytes 2359304 | tf_op jit(solution)/shard_map/ppermute | solution.py:236
  71.1 1.9 %collective-permute-start.7 = (f16[1024,384]{1,0:T(8,128)(2,1)S(1)}, f16[1024,384]{1,0:T(8,128)(2,1)S(1)}, u32[]{:S(2)}, u32[]{:S(2)}) collective-permute-start(f16[1024,384]{1,0:T(8,128)(2,1)S(1)} %add_convert_fusion.5), channel_id=1, source_target_pairs={{0,6},{32,38},{64,70},{96,102},{1,7},{33,39},{65,71},{97,103},{2,0... | collective-permute-start | bytes 2359304 | tf_op jit(solution)/shard_map/ppermute | solution.py:236
  72.9 10.5 %collective-permute-done.13 = f16[4096,256]{1,0:T(8,128)(2,1)S(1)} collective-permute-done((f16[4096,256]{1,0:T(8,128)(2,1)S(1)}, f16[4096,256]{1,0:T(8,128)(2,1)S(1)}, u32[]{:S(2)}, u32[]{:S(2)}) %collective-permute-start.13) | collective-permute-done | bytes 2097184 | tf_op jit(solution)/shard_map/ppermute | solution.py:236
  83.4 1.6 %collective-permute-start.14 = (f32[256,128]{1,0:T(8,128)S(1)}, f32[256,128]{1,0:T(8,128)S(1)}, u32[]{:S(2)}, u32[]{:S(2)}) collective-permute-start(f32[256,128]{1,0:T(8,128)S(1)} %add.313), channel_id=1, source_target_pairs={{0,64},{32,96},{64,0},{96,32},{1,65},{33,97},{65,1},{97,33},{2,66}... | collective-permute-start | bytes 393224 | tf_op jit(solution)/shard_map/ppermute | solution.py:236
  86.3 1.5 %convert_add_fusion.2 = f32[1024,384]{1,0:T(8,128)S(1)} fusion(f32[1024,384]{1,0:T(8,128)S(1)} %get-tuple-element.104, f16[2048,384]{1,0:T(8,128)(2,1)} %collective-permute-done.4), kind=kLoop, calls=%fused_computation.8 | loop fusion | flops 786432 | bytes 3932160 | tf_op jit(solution)/shard_map/add | solution.py:380
  87.8 1.4 convert_add_fusion.1
  89.2 0.7 add_convert_fusion
  91.8 2.9 %collective-permute-start.15 = (f16[4,256,384]{2,1,0:T(8,128)(2,1)S(1)}, f16[4,256,384]{2,1,0:T(8,128)(2,1)S(1)}, u32[]{:S(2)}, u32[]{:S(2)}) collective-permute-start(f16[4,256,384]{2,1,0:T(8,128)(2,1)S(1)} %dynamic-slice_bitcast_fusion), channel_id=1, source_target_pairs={{0,1},{32,33},{64,65},{96,97},{1,0},{33,32},{65,64},{97,96},{2,3},... | collective-permute-start | bytes 2359304 | tf_op jit(solution)/shard_map/ppermute | solution.py:236
  94.7 2.0 %collective-permute-start.21 = (f16[1024,256]{1,0:T(8,128)(2,1)S(1)}, f16[1024,256]{1,0:T(8,128)(2,1)S(1)}, u32[]{:S(2)}, u32[]{:S(2)}) collective-permute-start(f16[1024,256]{1,0:T(8,128)(2,1)S(1)} %pad_maximum_fusion.2), channel_id=1, source_target_pairs={{0,24},{32,56},{64,88},{96,120},{1,25},{33,57},{65,89},{97,121},{2... | collective-permute-start | bytes 1572872 | tf_op jit(solution)/shard_map/ppermute | solution.py:236
  96.7 3.0 %collective-permute-start.8 = (f16[512,384]{1,0:T(8,128)(2,1)S(1)}, f16[512,384]{1,0:T(8,128)(2,1)S(1)}, u32[]{:S(2)}, u32[]{:S(2)}) collective-permute-start(f16[512,384]{1,0:T(8,128)(2,1)S(1)} %get-tuple-element.98), channel_id=1, source_target_pairs={{0,6},{32,38},{64,70},{96,102},{1,7},{33,39},{65,71},{97,103},{2,0... | collective-permute-start | bytes 1179656 | tf_op jit(solution)/shard_map/ppermute | solution.py:236
  99.9 1.5 %collective-permute-done.10 = f16[512,384]{1,0:T(8,128)(2,1)S(1)} collective-permute-done((f16[512,384]{1,0:T(8,128)(2,1)S(1)}, f16[512,384]{1,0:T(8,128)(2,1)S(1)}, u32[]{:S(2)}, u32[]{:S(2)}) %collective-permute-start.10) | collective-permute-done | bytes 393248 | tf_op jit(solution)/shard_map/ppermute | solution.py:236
  101.5 4.4 %collective-permute-done.8 = f16[512,384]{1,0:T(8,128)(2,1)S(1)} collective-permute-done((f16[512,384]{1,0:T(8,128)(2,1)S(1)}, f16[512,384]{1,0:T(8,128)(2,1)S(1)}, u32[]{:S(2)}, u32[]{:S(2)}) %collective-permute-start.8) | collective-permute-done | bytes 393248 | tf_op jit(solution)/shard_map/ppermute | solution.py:236
  106.0 1.1 collective-permute-start.11
  107.1 2.8 %collective-permute-start.12 = (f16[256,384]{1,0:T(8,128)(2,1)S(1)}, f16[256,384]{1,0:T(8,128)(2,1)S(1)}, u32[]{:S(2)}, u32[]{:S(2)}) collective-permute-start(f16[256,384]{1,0:T(8,128)(2,1)S(1)} %get-tuple-element.102), channel_id=1, source_target_pairs={{0,6},{32,38},{64,70},{96,102},{1,7},{33,39},{65,71},{97,103},{2,0... | collective-permute-start | bytes 589832 | tf_op jit(solution)/shard_map/ppermute | solution.py:236
  110.5 3.2 %collective-permute-start.22 = (f16[512,256]{1,0:T(8,128)(2,1)S(1)}, f16[512,256]{1,0:T(8,128)(2,1)S(1)}, u32[]{:S(2)}, u32[]{:S(2)}) collective-permute-start(f16[512,256]{1,0:T(8,128)(2,1)S(1)} %get-tuple-element.122), channel_id=1, source_target_pairs={{0,24},{32,56},{64,88},{96,120},{1,25},{33,57},{65,89},{97,121},{2... | collective-permute-start | bytes 786440 | tf_op jit(solution)/shard_map/ppermute | solution.py:236
  114.6 3.4 %collective-permute-done.19 = f16[512,256]{1,0:T(8,128)(2,1)S(1)} collective-permute-done((f16[512,256]{1,0:T(8,128)(2,1)S(1)}, f16[512,256]{1,0:T(8,128)(2,1)S(1)}, u32[]{:S(2)}, u32[]{:S(2)}) %collective-permute-start.19) | collective-permute-done | bytes 262176 | tf_op jit(solution)/shard_map/ppermute | solution.py:236
  118.5 0.8 collective-permute-start.16
  119.3 0.9 collective-permute-start.25
  120.4 3.0 %collective-permute-start.23 = (f16[256,384]{1,0:T(8,128)(2,1)S(1)}, f16[256,384]{1,0:T(8,128)(2,1)S(1)}, u32[]{:S(2)}, u32[]{:S(2)}) collective-permute-start(f16[256,384]{1,0:T(8,128)(2,1)S(1)} %get-tuple-element.123), channel_id=1, source_target_pairs={{0,24},{32,56},{64,88},{96,120},{1,25},{33,57},{65,89},{97,121},{2... | collective-permute-start | bytes 589832 | tf_op jit(solution)/shard_map/ppermute | solution.py:236
  123.4 1.5 %collective-permute-start.17 = (f16[256,384]{1,0:T(8,128)(2,1)S(1)}, f16[256,384]{1,0:T(8,128)(2,1)S(1)}, u32[]{:S(2)}, u32[]{:S(2)}) collective-permute-start(f16[256,384]{1,0:T(8,128)(2,1)S(1)} %get-tuple-element.151), channel_id=1, source_target_pairs={{0,16},{32,48},{64,80},{96,112},{1,17},{33,49},{65,81},{97,113},{2... | collective-permute-start | bytes 589832 | tf_op jit(solution)/shard_map/ppermute | solution.py:236
  124.9 2.0 %outer_step.1 = (f32[256,1024]{1,0:T(8,128)}, f32[256,1024]{1,0:T(8,128)}, f32[256,128]{1,0:T(8,128)S(1)}) custom-call(s32[1]{0:T(128)S(6)} %copy.15.fragment, f32[256,1024]{1,0:T(8,128)S(1)} %copy-done.2, f32[256,1024]{1,0:T(8,128)S(1)} %copy-done.5, f32[256,128]{1,0:T(8,128)S(1)} %broadcast_multiply_fusion.drift), custom_call_target="tpu_custom_call" | custom-call | flops 1 | bytes 1 | tf_op jit(solution)/shard_map/outer_step/pallas_call | solution.py:261
  127.0 3.1 %collective-permute-start.24 = (f16[256,256]{1,0:T(8,128)(2,1)S(1)}, f16[256,256]{1,0:T(8,128)(2,1)S(1)}, u32[]{:S(2)}, u32[]{:S(2)}) collective-permute-start(f16[256,256]{1,0:T(8,128)(2,1)S(1)} %get-tuple-element.124), channel_id=1, source_target_pairs={{0,4},{32,36},{64,68},{96,100},{1,5},{33,37},{65,69},{97,101},{2,6... | collective-permute-start | bytes 393224 | tf_op jit(solution)/shard_map/ppermute | solution.py:236
  130.1 0.8 collective-permute-start.26
  131.1 2.5 %collective-permute-done.24 = f16[256,256]{1,0:T(8,128)(2,1)S(1)} collective-permute-done((f16[256,256]{1,0:T(8,128)(2,1)S(1)}, f16[256,256]{1,0:T(8,128)(2,1)S(1)}, u32[]{:S(2)}, u32[]{:S(2)}) %collective-permute-start.24) | collective-permute-done | bytes 131104 | tf_op jit(solution)/shard_map/ppermute | solution.py:236
  133.6 1.6 %collective-permute-done.26 = f16[256,256]{1,0:T(8,128)(2,1)S(1)} collective-permute-done((f16[256,256]{1,0:T(8,128)(2,1)S(1)}, f16[256,256]{1,0:T(8,128)(2,1)S(1)}, u32[]{:S(2)}, u32[]{:S(2)}) %collective-permute-start.26) | collective-permute-done | bytes 131104 | tf_op jit(solution)/shard_map/ppermute | solution.py:236
  135.2 2.4 %inner_step.1 = (f32[256,1024]{1,0:T(8,128)}, f32[256,1024]{1,0:T(8,128)}, f32[256,1024]{1,0:T(8,128)}) custom-call(s32[1]{0:T(128)S(6)} %copy.15.fragment, f32[256,384]{1,0:T(8,128)S(1)} %bitcast_add_fusion.grad_a, f32[256,384]{1,0:T(8,128)S(1)} %fusion.4.grad_b, f32[256,256]{1,0:T(8,128)S(1)} %fusion.7.grad_c, f32[256,1024]{1,0:T(8,128)S(1)} %bitcast.122, ...), custom_call_target="tpu_custom_call" | custom-call | flops 1 | bytes 1 | tf_op jit(solution)/shard_map/inner_step/pallas_call | solution.py:305
  (81 shorter events, 7.1 us)
Async XLA Ops:
  16.8 2.5 %copy-start = (f32[4096,256]{1,0:T(8,128)}, f32[4096,256]{1,0:T(8,128)S(1)}, u32[]{:S(2)}) copy-start(f32[4096,256]{1,0:T(8,128)S(1)} %get-tuple-element.79) | copy-start | bytes 12582916
  19.3 38.8 %collective-permute-start.1 = (f16[2048,384]{1,0:T(8,128)(2,1)}, f16[2048,384]{1,0:T(8,128)(2,1)}, u32[]{:S(2)}, u32[]{:S(2)}) collective-permute-start(f16[2048,384]{1,0:T(8,128)(2,1)} %convert_element_type.226), channel_id=1, source_target_pairs={{0,8},{32,40},{64,72},{96,104},{1,9},{33,41},{65,73},{97,105},{2,1... | collective-permute-start | bytes 4718600 | tf_op jit(solution)/shard_map/ppermute | solution.py:236
  22.8 36.8 %collective-permute-start.2 = (f16[2048,384]{1,0:T(8,128)(2,1)}, f16[2048,384]{1,0:T(8,128)(2,1)}, u32[]{:S(2)}, u32[]{:S(2)}) collective-permute-start(f16[2048,384]{1,0:T(8,128)(2,1)} %convert_element_type.227), channel_id=1, source_target_pairs={{0,24},{32,56},{64,88},{96,120},{1,25},{33,57},{65,89},{97,121},{2... | collective-permute-start | bytes 4718600 | tf_op jit(solution)/shard_map/ppermute | solution.py:236
  26.3 2.1 %copy-start.1 = (f32[1,256,1024]{2,1,0:T(8,128)S(1)}, f32[1,256,1024]{2,1,0:T(8,128)}, u32[]{:S(2)}) copy-start(f32[1,256,1024]{2,1,0:T(8,128)} %param.10) | copy-start | bytes 3145732
  26.3 2.1 %copy-start.2 = (f32[256,1024]{1,0:T(8,128)S(1)}, f32[256,1024]{1,0:T(8,128)}, u32[]{:S(2)}) copy-start(f32[256,1024]{1,0:T(8,128)} %anchor.1) | copy-start | bytes 3145732
  28.4 3.7 %collective-permute-start = (f32[256,128]{1,0:T(8,128)S(1)}, f32[256,128]{1,0:T(8,128)S(1)}, u32[]{:S(2)}, u32[]{:S(2)}) collective-permute-start(f32[256,128]{1,0:T(8,128)S(1)} %bitcast_subtract_fusion), channel_id=1, source_target_pairs={{0,32},{32,0},{64,96},{96,64},{1,33},{33,1},{65,97},{97,65},{2,34}... | collective-permute-start | bytes 393224 | tf_op jit(solution)/shard_map/ppermute | solution.py:236
  28.5 38.3 %collective-permute-start.3 = (f16[2048,384]{1,0:T(8,128)(2,1)}, f16[2048,384]{1,0:T(8,128)(2,1)}, u32[]{:S(2)}, u32[]{:S(2)}) collective-permute-start(f16[2048,384]{1,0:T(8,128)(2,1)} %convert_element_type.228), channel_id=1, source_target_pairs={{0,2},{32,34},{64,66},{96,98},{1,3},{33,35},{65,67},{97,99},{2,4},... | collective-permute-start | bytes 4718600 | tf_op jit(solution)/shard_map/ppermute | solution.py:236
  30.3 37.9 %collective-permute-start.4 = (f16[2048,384]{1,0:T(8,128)(2,1)}, f16[2048,384]{1,0:T(8,128)(2,1)}, u32[]{:S(2)}, u32[]{:S(2)}) collective-permute-start(f16[2048,384]{1,0:T(8,128)(2,1)} %convert_element_type.229), channel_id=1, source_target_pairs={{0,6},{32,38},{64,70},{96,102},{1,7},{33,39},{65,71},{97,103},{2,0... | collective-permute-start | bytes 4718600 | tf_op jit(solution)/shard_map/ppermute | solution.py:236
  34.6 48.8 %collective-permute-start.13 = (f16[4096,256]{1,0:T(8,128)(2,1)S(1)}, f16[4096,256]{1,0:T(8,128)(2,1)S(1)}, u32[]{:S(2)}, u32[]{:S(2)}) collective-permute-start(f16[4096,256]{1,0:T(8,128)(2,1)S(1)} %convert_element_type.230), channel_id=1, source_target_pairs={{0,1},{32,33},{64,65},{96,97},{1,0},{33,32},{65,64},{97,96},{2,3},... | collective-permute-start | bytes 6291464 | tf_op jit(solution)/shard_map/ppermute | solution.py:236
  49.8 2.8 %copy-start.7 = (f32[2048,384]{1,0:T(8,128)S(1)}, f32[2048,384]{1,0:T(8,128)}, u32[]{:S(2)}) copy-start(f32[2048,384]{1,0:T(8,128)} %get-tuple-element.103) | copy-start | bytes 9437188
  61.0 24.3 %collective-permute-start.6 = (f16[1024,384]{1,0:T(8,128)(2,1)S(1)}, f16[1024,384]{1,0:T(8,128)(2,1)S(1)}, u32[]{:S(2)}, u32[]{:S(2)}) collective-permute-start(f16[1024,384]{1,0:T(8,128)(2,1)S(1)} %add_convert_fusion.7), channel_id=1, source_target_pairs={{0,24},{32,56},{64,88},{96,120},{1,25},{33,57},{65,89},{97,121},{2... | collective-permute-start | bytes 2359304 | tf_op jit(solution)/shard_map/ppermute | solution.py:236
  64.0 21.0 %collective-permute-start.5 = (f16[1024,384]{1,0:T(8,128)(2,1)S(1)}, f16[1024,384]{1,0:T(8,128)(2,1)S(1)}, u32[]{:S(2)}, u32[]{:S(2)}) collective-permute-start(f16[1024,384]{1,0:T(8,128)(2,1)S(1)} %add_convert_fusion.8), channel_id=1, source_target_pairs={{0,8},{32,40},{64,72},{96,104},{1,9},{33,41},{65,73},{97,105},{2,1... | collective-permute-start | bytes 2359304 | tf_op jit(solution)/shard_map/ppermute | solution.py:236
  69.6 20.8 %collective-permute-start.9 = (f16[1024,384]{1,0:T(8,128)(2,1)S(1)}, f16[1024,384]{1,0:T(8,128)(2,1)S(1)}, u32[]{:S(2)}, u32[]{:S(2)}) collective-permute-start(f16[1024,384]{1,0:T(8,128)(2,1)S(1)} %add_convert_fusion.6), channel_id=1, source_target_pairs={{0,2},{32,34},{64,66},{96,98},{1,3},{33,35},{65,67},{97,99},{2,4},... | collective-permute-start | bytes 2359304 | tf_op jit(solution)/shard_map/ppermute | solution.py:236
  71.1 19.9 %collective-permute-start.7 = (f16[1024,384]{1,0:T(8,128)(2,1)S(1)}, f16[1024,384]{1,0:T(8,128)(2,1)S(1)}, u32[]{:S(2)}, u32[]{:S(2)}) collective-permute-start(f16[1024,384]{1,0:T(8,128)(2,1)S(1)} %add_convert_fusion.5), channel_id=1, source_target_pairs={{0,6},{32,38},{64,70},{96,102},{1,7},{33,39},{65,71},{97,103},{2,0... | collective-permute-start | bytes 2359304 | tf_op jit(solution)/shard_map/ppermute | solution.py:236
  83.4 8.2 %collective-permute-start.14 = (f32[256,128]{1,0:T(8,128)S(1)}, f32[256,128]{1,0:T(8,128)S(1)}, u32[]{:S(2)}, u32[]{:S(2)}) collective-permute-start(f32[256,128]{1,0:T(8,128)S(1)} %add.313), channel_id=1, source_target_pairs={{0,64},{32,96},{64,0},{96,32},{1,65},{33,97},{65,1},{97,33},{2,66}... | collective-permute-start | bytes 393224 | tf_op jit(solution)/shard_map/ppermute | solution.py:236
  86.3 2.9 %copy-start.6 = (f32[4096,256]{1,0:T(8,128)S(1)}, f32[4096,256]{1,0:T(8,128)}, u32[]{:S(2)}) copy-start(f32[4096,256]{1,0:T(8,128)} %get-tuple-element.107) | copy-start | bytes 12582916
  90.6 10.8 %collective-permute-start.10 = (f16[512,384]{1,0:T(8,128)(2,1)S(1)}, f16[512,384]{1,0:T(8,128)(2,1)S(1)}, u32[]{:S(2)}, u32[]{:S(2)}) collective-permute-start(f16[512,384]{1,0:T(8,128)(2,1)S(1)} %get-tuple-element.100), channel_id=1, source_target_pairs={{0,2},{32,34},{64,66},{96,98},{1,3},{33,35},{65,67},{97,99},{2,4},... | collective-permute-start | bytes 1179656 | tf_op jit(solution)/shard_map/ppermute | solution.py:236
  91.8 22.4 %collective-permute-start.15 = (f16[4,256,384]{2,1,0:T(8,128)(2,1)S(1)}, f16[4,256,384]{2,1,0:T(8,128)(2,1)S(1)}, u32[]{:S(2)}, u32[]{:S(2)}) collective-permute-start(f16[4,256,384]{2,1,0:T(8,128)(2,1)S(1)} %dynamic-slice_bitcast_fusion), channel_id=1, source_target_pairs={{0,1},{32,33},{64,65},{96,97},{1,0},{33,32},{65,64},{97,96},{2,3},... | collective-permute-start | bytes 2359304 | tf_op jit(solution)/shard_map/ppermute | solution.py:236
  94.7 15.5 %collective-permute-start.21 = (f16[1024,256]{1,0:T(8,128)(2,1)S(1)}, f16[1024,256]{1,0:T(8,128)(2,1)S(1)}, u32[]{:S(2)}, u32[]{:S(2)}) collective-permute-start(f16[1024,256]{1,0:T(8,128)(2,1)S(1)} %pad_maximum_fusion.2), channel_id=1, source_target_pairs={{0,24},{32,56},{64,88},{96,120},{1,25},{33,57},{65,89},{97,121},{2... | collective-permute-start | bytes 1572872 | tf_op jit(solution)/shard_map/ppermute | solution.py:236
  96.7 13.3 %collective-permute-start.18 = (f16[1024,256]{1,0:T(8,128)(2,1)S(1)}, f16[1024,256]{1,0:T(8,128)(2,1)S(1)}, u32[]{:S(2)}, u32[]{:S(2)}) collective-permute-start(f16[1024,256]{1,0:T(8,128)(2,1)S(1)} %pad_maximum_fusion.3), channel_id=1, source_target_pairs={{0,8},{32,40},{64,72},{96,104},{1,9},{33,41},{65,73},{97,105},{2,1... | collective-permute-start | bytes 1572872 | tf_op jit(solution)/shard_map/ppermute | solution.py:236
  96.7 9.2 %collective-permute-start.8 = (f16[512,384]{1,0:T(8,128)(2,1)S(1)}, f16[512,384]{1,0:T(8,128)(2,1)S(1)}, u32[]{:S(2)}, u32[]{:S(2)}) collective-permute-start(f16[512,384]{1,0:T(8,128)(2,1)S(1)} %get-tuple-element.98), channel_id=1, source_target_pairs={{0,6},{32,38},{64,70},{96,102},{1,7},{33,39},{65,71},{97,103},{2,0... | collective-permute-start | bytes 1179656 | tf_op jit(solution)/shard_map/ppermute | solution.py:236
  106.0 7.8 %collective-permute-start.11 = (f16[256,384]{1,0:T(8,128)(2,1)S(1)}, f16[256,384]{1,0:T(8,128)(2,1)S(1)}, u32[]{:S(2)}, u32[]{:S(2)}) collective-permute-start(f16[256,384]{1,0:T(8,128)(2,1)S(1)} %get-tuple-element.101), channel_id=1, source_target_pairs={{0,2},{32,34},{64,66},{96,98},{1,3},{33,35},{65,67},{97,99},{2,4},... | collective-permute-start | bytes 589832 | tf_op jit(solution)/shard_map/ppermute | solution.py:236
  107.1 6.8 %collective-permute-start.12 = (f16[256,384]{1,0:T(8,128)(2,1)S(1)}, f16[256,384]{1,0:T(8,128)(2,1)S(1)}, u32[]{:S(2)}, u32[]{:S(2)}) collective-permute-start(f16[256,384]{1,0:T(8,128)(2,1)S(1)} %get-tuple-element.102), channel_id=1, source_target_pairs={{0,6},{32,38},{64,70},{96,102},{1,7},{33,39},{65,71},{97,103},{2,0... | collective-permute-start | bytes 589832 | tf_op jit(solution)/shard_map/ppermute | solution.py:236
  110.4 7.7 %collective-permute-start.19 = (f16[512,256]{1,0:T(8,128)(2,1)S(1)}, f16[512,256]{1,0:T(8,128)(2,1)S(1)}, u32[]{:S(2)}, u32[]{:S(2)}) collective-permute-start(f16[512,256]{1,0:T(8,128)(2,1)S(1)} %get-tuple-element.119), channel_id=1, source_target_pairs={{0,8},{32,40},{64,72},{96,104},{1,9},{33,41},{65,73},{97,105},{2,1... | collective-permute-start | bytes 786440 | tf_op jit(solution)/shard_map/ppermute | solution.py:236
  110.5 7.6 %collective-permute-start.22 = (f16[512,256]{1,0:T(8,128)(2,1)S(1)}, f16[512,256]{1,0:T(8,128)(2,1)S(1)}, u32[]{:S(2)}, u32[]{:S(2)}) collective-permute-start(f16[512,256]{1,0:T(8,128)(2,1)S(1)} %get-tuple-element.122), channel_id=1, source_target_pairs={{0,24},{32,56},{64,88},{96,120},{1,25},{33,57},{65,89},{97,121},{2... | collective-permute-start | bytes 786440 | tf_op jit(solution)/shard_map/ppermute | solution.py:236
  118.2 6.7 %copy-start.5 = (f32[256,1024]{1,0:T(8,128)S(1)}, f32[256,1024]{1,0:T(8,128)}, u32[]{:S(2)}) copy-start(f32[256,1024]{1,0:T(8,128)} %momentum.1) | copy-start | bytes 3145732
  118.5 8.4 %collective-permute-start.16 = (f16[256,384]{1,0:T(8,128)(2,1)S(1)}, f16[256,384]{1,0:T(8,128)(2,1)S(1)}, u32[]{:S(2)}, u32[]{:S(2)}) collective-permute-start(f16[256,384]{1,0:T(8,128)(2,1)S(1)} %fusion.8), channel_id=1, source_target_pairs={{0,1},{32,33},{64,65},{96,97},{1,0},{33,32},{65,64},{97,96},{2,3},... | collective-permute-start | bytes 589832 | tf_op jit(solution)/shard_map/ppermute | solution.py:236
  119.3 11.8 %collective-permute-start.25 = (f16[256,256]{1,0:T(8,128)(2,1)S(1)}, f16[256,256]{1,0:T(8,128)(2,1)S(1)}, u32[]{:S(2)}, u32[]{:S(2)}) collective-permute-start(f16[256,256]{1,0:T(8,128)(2,1)S(1)} %get-tuple-element.125), channel_id=1, source_target_pairs={{0,2},{32,34},{64,66},{96,98},{1,3},{33,35},{65,67},{97,99},{2,4},... | collective-permute-start | bytes 393224 | tf_op jit(solution)/shard_map/ppermute | solution.py:236
  120.2 9.9 %collective-permute-start.20 = (f16[256,384]{1,0:T(8,128)(2,1)S(1)}, f16[256,384]{1,0:T(8,128)(2,1)S(1)}, u32[]{:S(2)}, u32[]{:S(2)}) collective-permute-start(f16[256,384]{1,0:T(8,128)(2,1)S(1)} %get-tuple-element.120), channel_id=1, source_target_pairs={{0,8},{32,40},{64,72},{96,104},{1,9},{33,41},{65,73},{97,105},{2,1... | collective-permute-start | bytes 589832 | tf_op jit(solution)/shard_map/ppermute | solution.py:236
  120.4 10.5 %collective-permute-start.23 = (f16[256,384]{1,0:T(8,128)(2,1)S(1)}, f16[256,384]{1,0:T(8,128)(2,1)S(1)}, u32[]{:S(2)}, u32[]{:S(2)}) collective-permute-start(f16[256,384]{1,0:T(8,128)(2,1)S(1)} %get-tuple-element.123), channel_id=1, source_target_pairs={{0,24},{32,56},{64,88},{96,120},{1,25},{33,57},{65,89},{97,121},{2... | collective-permute-start | bytes 589832 | tf_op jit(solution)/shard_map/ppermute | solution.py:236
  123.4 7.5 %collective-permute-start.17 = (f16[256,384]{1,0:T(8,128)(2,1)S(1)}, f16[256,384]{1,0:T(8,128)(2,1)S(1)}, u32[]{:S(2)}, u32[]{:S(2)}) collective-permute-start(f16[256,384]{1,0:T(8,128)(2,1)S(1)} %get-tuple-element.151), channel_id=1, source_target_pairs={{0,16},{32,48},{64,80},{96,112},{1,17},{33,49},{65,81},{97,113},{2... | collective-permute-start | bytes 589832 | tf_op jit(solution)/shard_map/ppermute | solution.py:236
  126.9 8.3 %copy-start.3 = (f32[1,256,1024]{2,1,0:T(8,128)S(1)}, f32[1,256,1024]{2,1,0:T(8,128)}, u32[]{:S(2)}) copy-start(f32[1,256,1024]{2,1,0:T(8,128)} %param.11) | copy-start | bytes 3145732
  126.9 8.3 %copy-start.4 = (f32[1,256,1024]{2,1,0:T(8,128)S(1)}, f32[1,256,1024]{2,1,0:T(8,128)}, u32[]{:S(2)}) copy-start(f32[1,256,1024]{2,1,0:T(8,128)} %param.12) | copy-start | bytes 3145732
  127.0 6.6 %collective-permute-start.24 = (f16[256,256]{1,0:T(8,128)(2,1)S(1)}, f16[256,256]{1,0:T(8,128)(2,1)S(1)}, u32[]{:S(2)}, u32[]{:S(2)}) collective-permute-start(f16[256,256]{1,0:T(8,128)(2,1)S(1)} %get-tuple-element.124), channel_id=1, source_target_pairs={{0,4},{32,36},{64,68},{96,100},{1,5},{33,37},{65,69},{97,101},{2,6... | collective-permute-start | bytes 393224 | tf_op jit(solution)/shard_map/ppermute | solution.py:236
  130.1 5.0 %collective-permute-start.26 = (f16[256,256]{1,0:T(8,128)(2,1)S(1)}, f16[256,256]{1,0:T(8,128)(2,1)S(1)}, u32[]{:S(2)}, u32[]{:S(2)}) collective-permute-start(f16[256,256]{1,0:T(8,128)(2,1)S(1)} %get-tuple-element.127), channel_id=1, source_target_pairs={{0,6},{32,38},{64,70},{96,102},{1,7},{33,39},{65,71},{97,103},{2,0... | collective-permute-start | bytes 393224 | tf_op jit(solution)/shard_map/ppermute | solution.py:236
where the time goes:
time: 138 us
  starting transfers between devices  44.6 us (32%)
  Pallas kernels  32.5 us (24%)
  waiting for transfers between devices  29.5 us (21%)
  other arithmetic  24 us (17%)
  local copies, waits for them, and re-layouts  5.42 us (4%)
  between operations  1.79 us (1%)
    ppermute x27, starting transfers between devices, send(): got = lax.ppermute(value, AXES, pairs_of(**CHANNELS[step]))  44.6 us
    ppermute x27, waiting for transfers between devices, send(): got = lax.ppermute(value, AXES, pairs_of(**CHANNELS[step]))  29.5 us
    pallas_call x1, Pallas kernels, dot_first(): pl.pallas_call(first_kernel, in_specs=[SMEM_SPEC, ANY_SPEC, ANY_SPEC], ou...  16.1 us
    pallas_call x1, Pallas kernels, dot_rest(): pl.pallas_call(rest_kernel, in_specs=[SMEM_SPEC, ANY_SPEC, ANY_SPEC], out...  12 us
    convert_element_type x4, other arithmetic, per_device(): term = order.ran(order.after(term).astype(SENT))  5.84 us
    add x4, other arithmetic, near(): value = order.after(half(own[part])) + wide(half(first[axis + way]))  5.62 us
    slice x6, local copies, waits for them, and re-layouts, low(): return value[:value.shape[0] // 2]  2.96 us
    convert_element_type x2, other arithmetic, per_device(): second[axis + '-'] = order.send(order.ran(term.astype(SENT)), axis + '-')  2.78 us
  transfers between devices with their start and end apart: 27, of which 8 were waited for; matrix products, arithmetic and copies ran while one was open for 19% of the time, Pallas kernels for 10%

commit v1 on v0

--- a/solution.py
+++ b/solution.py
@@ -125,64 +125,86 @@
             pltpu.SemaphoreType.DMA((2,)),
             pltpu.SemaphoreType.DMA((4,)),
         ],
-        compiler_params=pltpu.CompilerParams(vmem_limit_bytes=16 << 20),
+        compiler_params=pltpu.CompilerParams(vmem_limit_bytes=13 << 20),
         cost_estimate=SHORT,
         name="dot_rest",
     )(ids, in_hbm(acts), in_hbm(cots))
 
 
 def first_kernel(ids, acts, cots, *refs):
-    firsts, (mine, other) = refs[:4], refs[4:6]
-    held, cots_here, mine_here, sems, cots_sems, back_sems = refs[6:]
-    own = ids[24]
+    firsts, (held, cots_here, sems, cots_sems) = refs[:4], refs[4:]
     copies = []
-    for k, cut in enumerate((slice(0, WIDE), slice(2 * WIDE, 1024), slice(WIDE, 2 * WIDE))):
-        copies.append(pltpu.make_async_copy(cots.at[:, cut], cots_here.at[:, cut], cots_sems.at[k]))
+    for part in range(2):
+        cut = slice(part * WIDE, (part + 1) * WIDE)
+        copies.append(
+            pltpu.make_async_copy(cots.at[:, cut], cots_here.at[:, cut], cots_sems.at[part])
+        )
         copies[-1].start()
-    back = []
-    for i, left in streamed(acts, ids, held, sems, 12):
-        if i == 0:
-            for copy in copies:
-                copy.wait()
-        if i < 4 or i >= 8:
-            part, k = (0, i) if i < 4 else (1, i - 8)
-            right = cots_here[:, part * WIDE : (part + 1) * WIDE]
-            row = k % 2 * PAIR
-            firsts[2 * part + k // 2][row : row + PAIR] = turned(left[...], right)
-        if i < 8:
-            for k in range(2):
-                rows = pl.ds(pl.multiple_of(ids[2 * i + k] * 256, 256), 256)
-                for to, side in ((mine_here, own), (other, 1 - own)):
-                    half = left[:, pl.ds(pl.multiple_of(k * BLOCK + side * 256, 256), 256)]
-                    to[rows] = turned(half, cots_here[:, 2 * WIDE :])
-                copy = pltpu.make_async_copy(
-                    mine_here.at[rows], mine.at[rows], back_sems.at[2 * i + k]
-                )
-                copy.start()
-                back.append(copy)
-    for copy in back:
-        copy.wait()
+    for i, left in streamed(acts, ids, held, sems, 8):
+        part, row = i // 4, i % 2 * PAIR
+        if i % 4 == 0:
+            copies[part].wait()
+        right = cots_here[:, part * WIDE : (part + 1) * WIDE]
+        firsts[i // 2][row : row + PAIR] = turned(left[...], right)
 
 
 def dot_first(ids, acts, cots):
-    half = (ROWS // 2, NARROW)
     return pl.pallas_call(
         first_kernel,
         in_specs=[SMEM_SPEC, ANY_SPEC, ANY_SPEC],
-        out_specs=[VMEM_SPEC] * 4 + [ANY_SPEC, VMEM_SPEC],
-        out_shape=[pltpu.VMEM((2 * PAIR, WIDE), jnp.float32)] * 4
-        + [pltpu.HBM(half, jnp.float32), pltpu.VMEM(half, jnp.float32)],
+        out_specs=[VMEM_SPEC] * 4,
+        out_shape=[pltpu.VMEM((2 * PAIR, WIDE), jnp.float32)] * 4,
         scratch_shapes=[
             pltpu.VMEM((SLOTS, TOK, PAIR), acts.dtype),
-            pltpu.VMEM(cots.shape, cots.dtype),
-            pltpu.VMEM(half, jnp.float32),
+            pltpu.VMEM((TOK, 2 * WIDE), cots.dtype),
             pltpu.SemaphoreType.DMA((SLOTS, 2)),
-            pltpu.SemaphoreType.DMA((3,)),
-            pltpu.SemaphoreType.DMA((16,)),
+            pltpu.SemaphoreType.DMA((2,)),
         ],
-        compiler_params=pltpu.CompilerParams(vmem_limit_bytes=14 << 20),
+        compiler_params=pltpu.CompilerParams(vmem_limit_bytes=10 << 20),
         cost_estimate=SHORT,
         name="dot_first",
+    )(ids, in_hbm(acts), in_hbm(cots))
+
+
+def pair_kernel(ids, acts, cots, mine, other, held, cots_here, mine_here, sems, own_sems):
+    count, own = ROWS // PAIR, ids[0]
+    copy = pltpu.make_async_copy(cots.at[:, 2 * WIDE :], cots_here, own_sems.at[count])
+    copy.start()
+    back = []
+    for i, left in streamed(acts, range(2 * count), held, sems, count):
+        if i == 0:
+            copy.wait()
+        for k in range(2):
+            for to, side in ((mine_here, own), (other, 1 - own)):
+                half = left[:, pl.ds(pl.multiple_of(k * BLOCK + side * 256, 256), 256)]
+                to[i * 512 + k * 256 : i * 512 + (k + 1) * 256] = turned(half, cots_here[...])
+        cut = pl.ds(i * 512, 512)
+        back.append(pltpu.make_async_copy(mine_here.at[cut], mine.at[cut], own_sems.at[i]))
+        back[-1].start()
+    for copy in back:
+        copy.wait()
+
+
+def dot_pairs(ids, acts, cots):
+    count = ROWS // PAIR
+    return pl.pallas_call(
+        pair_kernel,
+        in_specs=[SMEM_SPEC, ANY_SPEC, ANY_SPEC],
+        out_specs=[ANY_SPEC, VMEM_SPEC],
+        out_shape=[
+            pltpu.HBM((ROWS // 2, NARROW), jnp.float32),
+            pltpu.VMEM((ROWS // 2, NARROW), jnp.float32),
+        ],
+        scratch_shapes=[
+            pltpu.VMEM((SLOTS, TOK, PAIR), acts.dtype),
+            pltpu.VMEM((TOK, NARROW), cots.dtype),
+            pltpu.VMEM((ROWS // 2, NARROW), jnp.float32),
+            pltpu.SemaphoreType.DMA((SLOTS, 2)),
+            pltpu.SemaphoreType.DMA((1 + count,)),
+        ],
+        compiler_params=pltpu.CompilerParams(vmem_limit_bytes=10 << 20),
+        cost_estimate=SHORT,
+        name="dot_pairs",
     )(ids, in_hbm(acts), in_hbm(cots))
 
 
@@ -348,9 +370,8 @@
     axes = ((0, "z"), (1, "x"))
     first, second, relayed = {}, {}, {}
     ids = blocks(0, [(2, 0), (1, 1), (-1, 0), (2, 1)])
-    ids += blocks(0, [(0, 0), (0, 1), (1, 0), (-1, 1)])
     ids += blocks(1, [(2, 0), (1, 1), (-1, 0), (2, 1)])
-    *terms, mine_c, other_c = dot_first(jnp.stack(ids + [h]), acts, cots)
+    terms = dot_first(jnp.stack(ids), acts, cots)
     for term, channel in zip(terms, ("z+", "z-", "x+", "x-")):
         term = order.ran(order.after(term).astype(SENT))
         first[channel] = order.send(term, channel)
@@ -362,7 +383,8 @@
     drift = order.after(cut(anchor) - cut(weights))
     drift = drift + order.send(drift, "c", "rep")
 
-    other_c = order.ran(order.after(other_c, drift).astype(SENT))
+    mine_c, other_c = dot_pairs(order.after(h.reshape(1)), acts, cots)
+    other_c = order.ran(tie(other_c, order.last, drift).astype(SENT))
     got_c = order.send(other_c, "y")
 
     ids = []
@@ -373,11 +395,11 @@
     relayed.update(zip(("z+", "z-", "x+", "x-"), terms))
     own = own_a, own_b
 
-    def near(part):
+    def near(part, *others):
         axis = axes[part][1]
         halves = []
         for half, way in ((low, "-"), (high, "+")):
-            value = order.after(half(own[part])) + wide(half(first[axis + way]))
+            value = order.after(half(own[part]), *others) + wide(half(first[axis + way]))
             halves.append(order.ran(value))
         return halves
 
@@ -387,8 +409,6 @@
         second[axis + "+"] = order.send(order.ran(term.astype(SENT)), axis + "+")
         term = order.after(relayed[axis + "-"]) + wide(high(first[axis + "-"]))
         second[axis + "-"] = order.send(order.ran(term.astype(SENT)), axis + "-")
-        if part == 0:
-            nears.append(near(part))
 
     def at(array, position, axis=0):
         return lax.dynamic_index_in_dim(array, position & 3, axis, keepdims=False)
@@ -426,25 +446,25 @@
             sums.append(order.ran(value.astype(SENT)))
         return stack(*sums)
 
+    nears.append(near(0, second["z+"]))
     sum_a = total(0, nears[0]).reshape(RING, BLOCK, WIDE)
     term_a = lambda k, s=sum_a: at(s, x + k)
     first_a = ring_first(term_a, "x")
     nears.append(near(1))
-    drift = drift + order.send(tie(drift, got_c), "l", "rep")
+    sum_b = total(1, nears[1]).reshape(RING, 2, 256, WIDE)
+    sum_b = swap(sum_b, 1).astype(SENT)
     sum_c = (wide(got_c) + order.after(mine_c)).astype(SENT)
     sum_c = order.ran(sum_c).reshape(RING, 1024, NARROW)
     term_c = lambda k, s=sum_c: at(s, z + k)
     first_c = ring_first(term_c, "z")
-    sum_b = total(1, nears[1]).reshape(RING, 2, 256, WIDE)
-    sum_b = swap(sum_b, 1, drift).astype(SENT)
     sum_c = ring_second(term_c, "z", first_c).astype(SENT).reshape(RING, 256, NARROW)
     sum_a = ring_second(term_a, "x", first_a).reshape(2, 256, WIDE)
-    drift = tie(drift, sum_b) / groups
-    new_anchor, new_momentum, mix = outer_step(fragment, anchor, momentum, drift)
+    drift = drift + order.send(tie(drift, sum_b), "l", "rep")
+    new_anchor, new_momentum, mix = outer_step(fragment, anchor, momentum, drift / groups)
 
     grad_a = swap(sum_a, 0)
     grad_b = direct_sum(lambda k: at(sum_b, z + k), "z")
-    grad_c = direct_sum(lambda k, s=sum_c: at(s, x + k), "x", grad_a)
+    grad_c = direct_sum(lambda k, s=tie(sum_c, grad_a): at(s, x + k), "x")
     new_w, new_first, new_second = inner_step(
         fragment, grad_a, grad_b, grad_c,
         weights, first_moment[0], second_moment[0], mix,

time: 138 us -> 137 us (level)
  waiting for transfers between devices: 29.5 us -> 23.8 us
  Pallas kernels: 32.5 us -> 35.9 us
    pallas_call x0 -> x1, Pallas kernels: none -> 8.63 us  [dot_pairs(): pl.pallas_call(pair_kernel, in_specs=[SMEM_SPEC, ANY_SPEC, ANY_SPEC], out...]
    ppermute x27, waiting for transfers between devices: 29.5 us -> 23.8 us  [send(): got = lax.ppermute(value, AXES, pairs_of(**CHANNELS[step]))]
    pallas_call x1, Pallas kernels: 16.1 us -> 10.8 us  [dot_first(): pl.pallas_call(first_kernel, in_specs=[SMEM_SPEC, ANY_SPEC, ANY_SPEC], ou...]
    add x5 -> x4, other arithmetic: 5.64 us -> 5.39 us  [near(): order.after(half(own[part]), *others) + wide(half(first[axis + way]))]
  transfers between devices with their start and end apart: 27 -> 27, of which waited for: 8 -> 8; matrix products, arithmetic and copies ran while one was open for 19% -> 19% of each run, Pallas kernels for 10% -> 17%
where the time goes in v1:
time: 137 us
  starting transfers between devices  44.8 us (33%)
  Pallas kernels  35.9 us (26%)
  other arithmetic  23.8 us (17%)
  waiting for transfers between devices  23.8 us (17%)
  local copies, waits for them, and re-layouts  6.52 us (5%)
  between operations  1.77 us (1%)
    ppermute x27, starting transfers between devices, send(): got = lax.ppermute(value, AXES, pairs_of(**CHANNELS[step]))  44.8 us
    ppermute x27, waiting for transfers between devices, send(): got = lax.ppermute(value, AXES, pairs_of(**CHANNELS[step]))  23.8 us
    pallas_call x1, Pallas kernels, dot_rest(): pl.pallas_call(rest_kernel, in_specs=[SMEM_SPEC, ANY_SPEC, ANY_SPEC], out...  12 us
    pallas_call x1, Pallas kernels, dot_first(): pl.pallas_call(first_kernel, in_specs=[SMEM_SPEC, ANY_SPEC, ANY_SPEC], ou...  10.8 us
    pallas_call x1, Pallas kernels, dot_pairs(): pl.pallas_call(pair_kernel, in_specs=[SMEM_SPEC, ANY_SPEC, ANY_SPEC], out...  8.63 us
    convert_element_type x4, other arithmetic, per_device(): term = order.ran(order.after(term).astype(SENT))  5.67 us
    add x4, other arithmetic, near(): order.after(half(own[part]), *others) + wide(half(first[axis + way]))  5.39 us
    slice x6, local copies, waits for them, and re-layouts, low(): return value[:value.shape[0] // 2]  2.96 us
  transfers between devices with their start and end apart: 27, of which 8 were waited for; matrix products, arithmetic and copies ran while one was open for 19% of the time, Pallas kernels for 17%

profile of v1, /device:TPU:0, one launch (start us, length us, event | category | flops | bytes accessed | tf_op | source)
XLA Modules:
  0.0 136.6 jit_solution(10759909134193207455)
XLA Ops:
  0.8 10.8 %dot_first.1 = (f32[2048,384]{1,0:T(8,128)S(1)}, f32[2048,384]{1,0:T(8,128)S(1)}, f32[2048,384]{1,0:T(8,128)S(1)}, f32[2048,384]{1,0:T(8,128)S(1)}) custom-call(s32[16]{0:T(128)S(1)} %stack.135.ids, bf16[768,8192]{1,0:T(8,128)(2,1)} %acts.5, bf16[768,1024]{1,0:T(8,128)(2,1)} %cots.5), custom_call_target="tpu_custom_call" | custom-call | flops 1 | bytes 1 | tf_op jit(solution)/shard_map/dot_first/pallas_call | solution.py:152
  11.6 1.4 %convert_element_type.226 = f16[2048,384]{1,0:T(8,128)(2,1)} convert(f32[2048,384]{1,0:T(8,128)S(1)} %get-tuple-element.72) | non-fusion elementwise | flops 786432 | bytes 4718592 | tf_op jit(solution)/shard_map/convert_element_type | solution.py:376
  13.0 2.0 %collective-permute-start.1 = (f16[2048,384]{1,0:T(8,128)(2,1)}, f16[2048,384]{1,0:T(8,128)(2,1)}, u32[]{:S(2)}, u32[]{:S(2)}) collective-permute-start(f16[2048,384]{1,0:T(8,128)(2,1)} %convert_element_type.226), channel_id=1, source_target_pairs={{0,8},{32,40},{64,72},{96,104},{1,9},{33,41},{65,73},{97,105},{2,1... | collective-permute-start | bytes 4718600 | tf_op jit(solution)/shard_map/ppermute | solution.py:258
  15.0 1.4 %convert_element_type.227 = f16[2048,384]{1,0:T(8,128)(2,1)} convert(f32[2048,384]{1,0:T(8,128)S(1)} %get-tuple-element.73) | non-fusion elementwise | flops 786432 | bytes 4718592 | tf_op jit(solution)/shard_map/convert_element_type | solution.py:376
  16.4 2.1 %collective-permute-start.2 = (f16[2048,384]{1,0:T(8,128)(2,1)}, f16[2048,384]{1,0:T(8,128)(2,1)}, u32[]{:S(2)}, u32[]{:S(2)}) collective-permute-start(f16[2048,384]{1,0:T(8,128)(2,1)} %convert_element_type.227), channel_id=1, source_target_pairs={{0,24},{32,56},{64,88},{96,120},{1,25},{33,57},{65,89},{97,121},{2... | collective-permute-start | bytes 4718600 | tf_op jit(solution)/shard_map/ppermute | solution.py:258
  18.5 1.4 %convert_element_type.228 = f16[2048,384]{1,0:T(8,128)(2,1)} convert(f32[2048,384]{1,0:T(8,128)S(1)} %get-tuple-element.74) | non-fusion elementwise | flops 786432 | bytes 4718592 | tf_op jit(solution)/shard_map/convert_element_type | solution.py:376
  19.9 1.5 %collective-permute-start.3 = (f16[2048,384]{1,0:T(8,128)(2,1)}, f16[2048,384]{1,0:T(8,128)(2,1)}, u32[]{:S(2)}, u32[]{:S(2)}) collective-permute-start(f16[2048,384]{1,0:T(8,128)(2,1)} %convert_element_type.228), channel_id=1, source_target_pairs={{0,2},{32,34},{64,66},{96,98},{1,3},{33,35},{65,67},{97,99},{2,4},... | collective-permute-start | bytes 4718600 | tf_op jit(solution)/shard_map/ppermute | solution.py:258
  21.4 1.4 %convert_element_type.229 = f16[2048,384]{1,0:T(8,128)(2,1)} convert(f32[2048,384]{1,0:T(8,128)S(1)} %get-tuple-element.75) | non-fusion elementwise | flops 786432 | bytes 4718592 | tf_op jit(solution)/shard_map/convert_element_type | solution.py:376
  23.7 2.0 %collective-permute-start.4 = (f16[2048,384]{1,0:T(8,128)(2,1)}, f16[2048,384]{1,0:T(8,128)(2,1)}, u32[]{:S(2)}, u32[]{:S(2)}) collective-permute-start(f16[2048,384]{1,0:T(8,128)(2,1)} %convert_element_type.229), channel_id=1, source_target_pairs={{0,6},{32,38},{64,70},{96,102},{1,7},{33,39},{65,71},{97,103},{2,0... | collective-permute-start | bytes 4718600 | tf_op jit(solution)/shard_map/ppermute | solution.py:258
  25.7 8.6 %dot_pairs.1 = (f32[4096,256]{1,0:T(8,128)}, f32[4096,256]{1,0:T(8,128)S(1)}) custom-call(s32[1]{0:T(128)} %bitcast.16.ids, bf16[768,8192]{1,0:T(8,128)(2,1)} %acts.5, bf16[768,1024]{1,0:T(8,128)(2,1)} %cots.5), custom_call_target="tpu_custom_call" | custom-call | flops 1 | bytes 1 | tf_op jit(solution)/shard_map/dot_pairs/pallas_call | solution.py:190
  34.3 2.0 %copy-done = f32[4096,256]{1,0:T(8,128)} copy-done((f32[4096,256]{1,0:T(8,128)}, f32[4096,256]{1,0:T(8,128)S(1)}, u32[]{:S(2)}) %copy-start) | copy-done | bytes 4194328
  36.5 2.5 %convert_element_type.230 = f16[4096,256]{1,0:T(8,128)(2,1)S(1)} convert(f32[4096,256]{1,0:T(8,128)} %copy-done) | non-fusion elementwise | flops 1048576 | bytes 6291456 | tf_op jit(solution)/shard_map/convert_element_type | solution.py:387
  38.9 3.3 %collective-permute-start.13 = (f16[4096,256]{1,0:T(8,128)(2,1)S(1)}, f16[4096,256]{1,0:T(8,128)(2,1)S(1)}, u32[]{:S(2)}, u32[]{:S(2)}) collective-permute-start(f16[4096,256]{1,0:T(8,128)(2,1)S(1)} %convert_element_type.230), channel_id=1, source_target_pairs={{0,1},{32,33},{64,65},{96,97},{1,0},{33,32},{65,64},{97,96},{2,3},... | collective-permute-start | bytes 6291464 | tf_op jit(solution)/shard_map/ppermute | solution.py:258
  42.2 12.0 %dot_rest.1 = (f32[1024,384]{1,0:T(8,128)S(1)}, f32[1024,384]{1,0:T(8,128)S(1)}, f32[1024,384]{1,0:T(8,128)S(1)}, f32[1024,384]{1,0:T(8,128)S(1)}, f32[2048,384]{1,0:T(8,128)}, /*index=5*/f32[2048,384]{1,0:T(8,128)}) custom-call(s32[16]{0:T(128)S(1)} %stack.118.ids, bf16[768,8192]{1,0:T(8,128)(2,1)} %acts.5, bf16[768,1024]{1,0:T(8,128)(2,1)} %cots.5), custom_call_target="tpu_custom_call" | custom-call | flops 1 | bytes 1 | tf_op jit(solution)/shard_map/dot_rest/pallas_call | solution.py:114
  54.2 2.2 %fusion.10 = (f32[1024,384]{1,0:T(8,128)S(1)}, f32[1024,384]{1,0:T(8,128)S(1)}) fusion(f32[2048,384]{1,0:T(8,128)} %get-tuple-element.81), kind=kLoop, calls=%fused_computation.69 | loop fusion | bytes 6291456 | tf_op jit(solution)/shard_map/slice | solution.py:343
  57.2 1.4 %add_convert_fusion.8 = f16[1024,384]{1,0:T(8,128)(2,1)S(1)} fusion(f32[1024,384]{1,0:T(8,128)S(1)} %get-tuple-element.85, f16[2048,384]{1,0:T(8,128)(2,1)} %collective-permute-done.1), kind=kLoop, calls=%fused_computation.16 | loop fusion | flops 1179648 | bytes 3145728 | tf_op jit(solution)/shard_map/convert_element_type | solution.py:409
  58.7 1.4 %add_convert_fusion.7 = f16[1024,384]{1,0:T(8,128)(2,1)S(1)} fusion(f32[1024,384]{1,0:T(8,128)S(1)} %get-tuple-element.86, f16[2048,384]{1,0:T(8,128)(2,1)} %collective-permute-done.2), kind=kLoop, calls=%fused_computation.15 | loop fusion | flops 1179648 | bytes 3145728 | tf_op jit(solution)/shard_map/convert_element_type | solution.py:411
  60.1 3.5 %collective-permute-start.6 = (f16[1024,384]{1,0:T(8,128)(2,1)S(1)}, f16[1024,384]{1,0:T(8,128)(2,1)S(1)}, u32[]{:S(2)}, u32[]{:S(2)}) collective-permute-start(f16[1024,384]{1,0:T(8,128)(2,1)S(1)} %add_convert_fusion.7), channel_id=1, source_target_pairs={{0,24},{32,56},{64,88},{96,120},{1,25},{33,57},{65,89},{97,121},{2... | collective-permute-start | bytes 2359304 | tf_op jit(solution)/shard_map/ppermute | solution.py:258
  63.6 1.4 %add_convert_fusion.6 = f16[1024,384]{1,0:T(8,128)(2,1)S(1)} fusion(f32[1024,384]{1,0:T(8,128)S(1)} %get-tuple-element.87, f16[2048,384]{1,0:T(8,128)(2,1)} %collective-permute-done.3), kind=kLoop, calls=%fused_computation.14 | loop fusion | flops 1179648 | bytes 3145728 | tf_op jit(solution)/shard_map/convert_element_type | solution.py:409
  65.4 1.4 %add_convert_fusion.5 = f16[1024,384]{1,0:T(8,128)(2,1)S(1)} fusion(f32[1024,384]{1,0:T(8,128)S(1)} %get-tuple-element.88, f16[2048,384]{1,0:T(8,128)(2,1)} %collective-permute-done.4), kind=kLoop, calls=%fused_computation.13 | loop fusion | flops 1179648 | bytes 3145728 | tf_op jit(solution)/shard_map/convert_element_type | solution.py:411
  66.8 3.0 %collective-permute-start.7 = (f16[1024,384]{1,0:T(8,128)(2,1)S(1)}, f16[1024,384]{1,0:T(8,128)(2,1)S(1)}, u32[]{:S(2)}, u32[]{:S(2)}) collective-permute-start(f16[1024,384]{1,0:T(8,128)(2,1)S(1)} %add_convert_fusion.5), channel_id=1, source_target_pairs={{0,6},{32,38},{64,70},{96,102},{1,7},{33,39},{65,71},{97,103},{2,0... | collective-permute-start | bytes 2359304 | tf_op jit(solution)/shard_map/ppermute | solution.py:258
  69.8 9.3 %collective-permute-done.5 = f16[1024,384]{1,0:T(8,128)(2,1)S(1)} collective-permute-done((f16[1024,384]{1,0:T(8,128)(2,1)S(1)}, f16[1024,384]{1,0:T(8,128)(2,1)S(1)}, u32[]{:S(2)}, u32[]{:S(2)}) %collective-permute-start.5) | collective-permute-done | bytes 786464 | tf_op jit(solution)/shard_map/ppermute | solution.py:258
  79.0 1.4 %convert_add_fusion.4 = f32[1024,384]{1,0:T(8,128)S(1)} fusion(f32[1024,384]{1,0:T(8,128)S(1)} %get-tuple-element.90, f16[2048,384]{1,0:T(8,128)(2,1)} %collective-permute-done.2), kind=kLoop, calls=%fused_computation.12 | loop fusion | flops 786432 | bytes 3932160 | tf_op jit(solution)/shard_map/add | solution.py:402
  80.4 1.4 %convert_add_fusion.3 = f32[1024,384]{1,0:T(8,128)S(1)} fusion(f32[1024,384]{1,0:T(8,128)S(1)} %get-tuple-element.91, f16[2048,384]{1,0:T(8,128)(2,1)} %collective-permute-done.1), kind=kLoop, calls=%fused_computation.11 | loop fusion | flops 786432 | bytes 3932160 | tf_op jit(solution)/shard_map/add | solution.py:402
  83.1 1.3 convert_add_fusion.2
  84.4 1.4 %convert_add_fusion.1 = f32[1024,384]{1,0:T(8,128)S(1)} fusion(f32[1024,384]{1,0:T(8,128)S(1)} %get-tuple-element.106, f16[2048,384]{1,0:T(8,128)(2,1)} %collective-permute-done.3), kind=kLoop, calls=%fused_computation.7 | loop fusion | flops 786432 | bytes 3932160 | tf_op jit(solution)/shard_map/add | solution.py:402
  86.9 1.1 collective-permute-done.13
  88.0 3.2 %collective-permute-start.14 = (f16[4,256,384]{2,1,0:T(8,128)(2,1)S(1)}, f16[4,256,384]{2,1,0:T(8,128)(2,1)S(1)}, u32[]{:S(2)}, u32[]{:S(2)}) collective-permute-start(f16[4,256,384]{2,1,0:T(8,128)(2,1)S(1)} %dynamic-slice_bitcast_fusion), channel_id=1, source_target_pairs={{0,1},{32,33},{64,65},{96,97},{1,0},{33,32},{65,64},{97,96},{2,3},... | collective-permute-start | bytes 2359304 | tf_op jit(solution)/shard_map/ppermute | solution.py:258
  91.5 0.7 add_convert_fusion
  92.7 2.1 %collective-permute-start.20 = (f16[1024,256]{1,0:T(8,128)(2,1)S(1)}, f16[1024,256]{1,0:T(8,128)(2,1)S(1)}, u32[]{:S(2)}, u32[]{:S(2)}) collective-permute-start(f16[1024,256]{1,0:T(8,128)(2,1)S(1)} %pad_maximum_fusion.2), channel_id=1, source_target_pairs={{0,24},{32,56},{64,88},{96,120},{1,25},{33,57},{65,89},{97,121},{2... | collective-permute-start | bytes 1572872 | tf_op jit(solution)/shard_map/ppermute | solution.py:258
  94.8 2.9 %collective-permute-start.8 = (f16[512,384]{1,0:T(8,128)(2,1)S(1)}, f16[512,384]{1,0:T(8,128)(2,1)S(1)}, u32[]{:S(2)}, u32[]{:S(2)}) collective-permute-start(f16[512,384]{1,0:T(8,128)(2,1)S(1)} %get-tuple-element.98), channel_id=1, source_target_pairs={{0,6},{32,38},{64,70},{96,102},{1,7},{33,39},{65,71},{97,103},{2,0... | collective-permute-start | bytes 1179656 | tf_op jit(solution)/shard_map/ppermute | solution.py:258
  97.9 4.3 %collective-permute-done.10 = f16[512,384]{1,0:T(8,128)(2,1)S(1)} collective-permute-done((f16[512,384]{1,0:T(8,128)(2,1)S(1)}, f16[512,384]{1,0:T(8,128)(2,1)S(1)}, u32[]{:S(2)}, u32[]{:S(2)}) %collective-permute-start.10) | collective-permute-done | bytes 393248 | tf_op jit(solution)/shard_map/ppermute | solution.py:258
  102.3 2.2 %collective-permute-done.8 = f16[512,384]{1,0:T(8,128)(2,1)S(1)} collective-permute-done((f16[512,384]{1,0:T(8,128)(2,1)S(1)}, f16[512,384]{1,0:T(8,128)(2,1)S(1)}, u32[]{:S(2)}, u32[]{:S(2)}) %collective-permute-start.8) | collective-permute-done | bytes 393248 | tf_op jit(solution)/shard_map/ppermute | solution.py:258
  104.7 1.1 collective-permute-start.11
  105.8 2.8 %collective-permute-start.12 = (f16[256,384]{1,0:T(8,128)(2,1)S(1)}, f16[256,384]{1,0:T(8,128)(2,1)S(1)}, u32[]{:S(2)}, u32[]{:S(2)}) collective-permute-start(f16[256,384]{1,0:T(8,128)(2,1)S(1)} %get-tuple-element.102), channel_id=1, source_target_pairs={{0,6},{32,38},{64,70},{96,102},{1,7},{33,39},{65,71},{97,103},{2,0... | collective-permute-start | bytes 589832 | tf_op jit(solution)/shard_map/ppermute | solution.py:258
  109.1 3.2 %collective-permute-start.21 = (f16[512,256]{1,0:T(8,128)(2,1)S(1)}, f16[512,256]{1,0:T(8,128)(2,1)S(1)}, u32[]{:S(2)}, u32[]{:S(2)}) collective-permute-start(f16[512,256]{1,0:T(8,128)(2,1)S(1)} %get-tuple-element.120), channel_id=1, source_target_pairs={{0,24},{32,56},{64,88},{96,120},{1,25},{33,57},{65,89},{97,121},{2... | collective-permute-start | bytes 786440 | tf_op jit(solution)/shard_map/ppermute | solution.py:258
  113.1 0.8 collective-permute-start.26
  113.9 1.8 %collective-permute-start.15 = (f16[256,384]{1,0:T(8,128)(2,1)S(1)}, f16[256,384]{1,0:T(8,128)(2,1)S(1)}, u32[]{:S(2)}, u32[]{:S(2)}) collective-permute-start(f16[256,384]{1,0:T(8,128)(2,1)S(1)} %fusion.8), channel_id=1, source_target_pairs={{0,1},{32,33},{64,65},{96,97},{1,0},{33,32},{65,64},{97,96},{2,3},... | collective-permute-start | bytes 589832 | tf_op jit(solution)/shard_map/ppermute | solution.py:258
  115.8 1.1 collective-permute-done.18
  116.9 3.5 %collective-permute-start.22 = (f16[256,384]{1,0:T(8,128)(2,1)S(1)}, f16[256,384]{1,0:T(8,128)(2,1)S(1)}, u32[]{:S(2)}, u32[]{:S(2)}) collective-permute-start(f16[256,384]{1,0:T(8,128)(2,1)S(1)} %get-tuple-element.121), channel_id=1, source_target_pairs={{0,24},{32,56},{64,88},{96,120},{1,25},{33,57},{65,89},{97,121},{2... | collective-permute-start | bytes 589832 | tf_op jit(solution)/shard_map/ppermute | solution.py:258
  120.4 1.2 collective-permute-start.16
  122.0 2.0 %outer_step.1 = (f32[256,1024]{1,0:T(8,128)}, f32[256,1024]{1,0:T(8,128)}, f32[256,128]{1,0:T(8,128)S(1)}) custom-call(s32[1]{0:T(128)S(6)} %copy.15.fragment, f32[256,1024]{1,0:T(8,128)S(1)} %copy-done.2, f32[256,1024]{1,0:T(8,128)S(1)} %copy-done.5, f32[256,128]{1,0:T(8,128)S(1)} %add_multiply_fusion.drift), custom_call_target="tpu_custom_call" | custom-call | flops 1 | bytes 1 | tf_op jit(solution)/shard_map/outer_step/pallas_call | solution.py:283
  124.5 3.1 %collective-permute-start.25 = (f16[256,256]{1,0:T(8,128)(2,1)S(1)}, f16[256,256]{1,0:T(8,128)(2,1)S(1)}, u32[]{:S(2)}, u32[]{:S(2)}) collective-permute-start(f16[256,256]{1,0:T(8,128)(2,1)S(1)} %get-tuple-element.124), channel_id=1, source_target_pairs={{0,6},{32,38},{64,70},{96,102},{1,7},{33,39},{65,71},{97,103},{2,0... | collective-permute-start | bytes 393224 | tf_op jit(solution)/shard_map/ppermute | solution.py:258
  127.6 0.6 collective-permute-start.23
  128.3 2.2 %collective-permute-done.24 = f16[256,256]{1,0:T(8,128)(2,1)S(1)} collective-permute-done((f16[256,256]{1,0:T(8,128)(2,1)S(1)}, f16[256,256]{1,0:T(8,128)(2,1)S(1)}, u32[]{:S(2)}, u32[]{:S(2)}) %collective-permute-start.24) | collective-permute-done | bytes 131104 | tf_op jit(solution)/shard_map/ppermute | solution.py:258
  130.5 1.0 collective-permute-done.25
  131.5 2.6 %collective-permute-done.23 = f16[256,256]{1,0:T(8,128)(2,1)S(1)} collective-permute-done((f16[256,256]{1,0:T(8,128)(2,1)S(1)}, f16[256,256]{1,0:T(8,128)(2,1)S(1)}, u32[]{:S(2)}, u32[]{:S(2)}) %collective-permute-start.23) | collective-permute-done | bytes 131104 | tf_op jit(solution)/shard_map/ppermute | solution.py:258
  134.1 2.4 %inner_step.1 = (f32[256,1024]{1,0:T(8,128)}, f32[256,1024]{1,0:T(8,128)}, f32[256,1024]{1,0:T(8,128)}) custom-call(s32[1]{0:T(128)S(6)} %copy.15.fragment, f32[256,384]{1,0:T(8,128)S(1)} %bitcast_add_fusion.grad_a, f32[256,384]{1,0:T(8,128)S(1)} %fusion.4.grad_b, f32[256,256]{1,0:T(8,128)S(1)} %fusion.7.grad_c, f32[256,1024]{1,0:T(8,128)S(1)} %bitcast.122, ...), custom_call_target="tpu_custom_call" | custom-call | flops 1 | bytes 1 | tf_op jit(solution)/shard_map/inner_step/pallas_call | solution.py:327
  (81 shorter events, 7.5 us)
Async XLA Ops:
  13.0 44.3 %collective-permute-start.1 = (f16[2048,384]{1,0:T(8,128)(2,1)}, f16[2048,384]{1,0:T(8,128)(2,1)}, u32[]{:S(2)}, u32[]{:S(2)}) collective-permute-start(f16[2048,384]{1,0:T(8,128)(2,1)} %convert_element_type.226), channel_id=1, source_target_pairs={{0,8},{32,40},{64,72},{96,104},{1,9},{33,41},{65,73},{97,105},{2,1... | collective-permute-start | bytes 4718600 | tf_op jit(solution)/shard_map/ppermute | solution.py:258
  16.4 42.3 %collective-permute-start.2 = (f16[2048,384]{1,0:T(8,128)(2,1)}, f16[2048,384]{1,0:T(8,128)(2,1)}, u32[]{:S(2)}, u32[]{:S(2)}) collective-permute-start(f16[2048,384]{1,0:T(8,128)(2,1)} %convert_element_type.227), channel_id=1, source_target_pairs={{0,24},{32,56},{64,88},{96,120},{1,25},{33,57},{65,89},{97,121},{2... | collective-permute-start | bytes 4718600 | tf_op jit(solution)/shard_map/ppermute | solution.py:258
  19.9 43.7 %collective-permute-start.3 = (f16[2048,384]{1,0:T(8,128)(2,1)}, f16[2048,384]{1,0:T(8,128)(2,1)}, u32[]{:S(2)}, u32[]{:S(2)}) collective-permute-start(f16[2048,384]{1,0:T(8,128)(2,1)} %convert_element_type.228), channel_id=1, source_target_pairs={{0,2},{32,34},{64,66},{96,98},{1,3},{33,35},{65,67},{97,99},{2,4},... | collective-permute-start | bytes 4718600 | tf_op jit(solution)/shard_map/ppermute | solution.py:258
  21.4 2.1 %copy-start.1 = (f32[1,256,1024]{2,1,0:T(8,128)S(1)}, f32[1,256,1024]{2,1,0:T(8,128)}, u32[]{:S(2)}) copy-start(f32[1,256,1024]{2,1,0:T(8,128)} %param.10) | copy-start | bytes 3145732
  21.4 2.1 %copy-start.2 = (f32[256,1024]{1,0:T(8,128)S(1)}, f32[256,1024]{1,0:T(8,128)}, u32[]{:S(2)}) copy-start(f32[256,1024]{1,0:T(8,128)} %anchor.1) | copy-start | bytes 3145732
  23.6 12.8 %collective-permute-start = (f32[256,128]{1,0:T(8,128)S(1)}, f32[256,128]{1,0:T(8,128)S(1)}, u32[]{:S(2)}, u32[]{:S(2)}) collective-permute-start(f32[256,128]{1,0:T(8,128)S(1)} %bitcast_subtract_fusion), channel_id=1, source_target_pairs={{0,32},{32,0},{64,96},{96,64},{1,33},{33,1},{65,97},{97,65},{2,34}... | collective-permute-start | bytes 393224 | tf_op jit(solution)/shard_map/ppermute | solution.py:258
  23.7 41.7 %collective-permute-start.4 = (f16[2048,384]{1,0:T(8,128)(2,1)}, f16[2048,384]{1,0:T(8,128)(2,1)}, u32[]{:S(2)}, u32[]{:S(2)}) collective-permute-start(f16[2048,384]{1,0:T(8,128)(2,1)} %convert_element_type.229), channel_id=1, source_target_pairs={{0,6},{32,38},{64,70},{96,102},{1,7},{33,39},{65,71},{97,103},{2,0... | collective-permute-start | bytes 4718600 | tf_op jit(solution)/shard_map/ppermute | solution.py:258
  34.3 2.0 %copy-start = (f32[4096,256]{1,0:T(8,128)}, f32[4096,256]{1,0:T(8,128)S(1)}, u32[]{:S(2)}) copy-start(f32[4096,256]{1,0:T(8,128)S(1)} %get-tuple-element.79) | copy-start | bytes 12582916
  38.9 49.1 %collective-permute-start.13 = (f16[4096,256]{1,0:T(8,128)(2,1)S(1)}, f16[4096,256]{1,0:T(8,128)(2,1)S(1)}, u32[]{:S(2)}, u32[]{:S(2)}) collective-permute-start(f16[4096,256]{1,0:T(8,128)(2,1)S(1)} %convert_element_type.230), channel_id=1, source_target_pairs={{0,1},{32,33},{64,65},{96,97},{1,0},{33,32},{65,64},{97,96},{2,3},... | collective-permute-start | bytes 6291464 | tf_op jit(solution)/shard_map/ppermute | solution.py:258
  54.2 2.8 %copy-start.7 = (f32[2048,384]{1,0:T(8,128)S(1)}, f32[2048,384]{1,0:T(8,128)}, u32[]{:S(2)}) copy-start(f32[2048,384]{1,0:T(8,128)} %get-tuple-element.104) | copy-start | bytes 9437188
  58.6 20.4 %collective-permute-start.5 = (f16[1024,384]{1,0:T(8,128)(2,1)S(1)}, f16[1024,384]{1,0:T(8,128)(2,1)S(1)}, u32[]{:S(2)}, u32[]{:S(2)}) collective-permute-start(f16[1024,384]{1,0:T(8,128)(2,1)S(1)} %add_convert_fusion.8), channel_id=1, source_target_pairs={{0,8},{32,40},{64,72},{96,104},{1,9},{33,41},{65,73},{97,105},{2,1... | collective-permute-start | bytes 2359304 | tf_op jit(solution)/shard_map/ppermute | solution.py:258
  60.1 21.9 %collective-permute-start.6 = (f16[1024,384]{1,0:T(8,128)(2,1)S(1)}, f16[1024,384]{1,0:T(8,128)(2,1)S(1)}, u32[]{:S(2)}, u32[]{:S(2)}) collective-permute-start(f16[1024,384]{1,0:T(8,128)(2,1)S(1)} %add_convert_fusion.7), channel_id=1, source_target_pairs={{0,24},{32,56},{64,88},{96,120},{1,25},{33,57},{65,89},{97,121},{2... | collective-permute-start | bytes 2359304 | tf_op jit(solution)/shard_map/ppermute | solution.py:258
  65.0 20.7 %collective-permute-start.9 = (f16[1024,384]{1,0:T(8,128)(2,1)S(1)}, f16[1024,384]{1,0:T(8,128)(2,1)S(1)}, u32[]{:S(2)}, u32[]{:S(2)}) collective-permute-start(f16[1024,384]{1,0:T(8,128)(2,1)S(1)} %add_convert_fusion.6), channel_id=1, source_target_pairs={{0,2},{32,34},{64,66},{96,98},{1,3},{33,35},{65,67},{97,99},{2,4},... | collective-permute-start | bytes 2359304 | tf_op jit(solution)/shard_map/ppermute | solution.py:258
  66.8 19.3 %collective-permute-start.7 = (f16[1024,384]{1,0:T(8,128)(2,1)S(1)}, f16[1024,384]{1,0:T(8,128)(2,1)S(1)}, u32[]{:S(2)}, u32[]{:S(2)}) collective-permute-start(f16[1024,384]{1,0:T(8,128)(2,1)S(1)} %add_convert_fusion.5), channel_id=1, source_target_pairs={{0,6},{32,38},{64,70},{96,102},{1,7},{33,39},{65,71},{97,103},{2,0... | collective-permute-start | bytes 2359304 | tf_op jit(solution)/shard_map/ppermute | solution.py:258
  86.3 5.2 %copy-start.6 = (f32[4096,256]{1,0:T(8,128)S(1)}, f32[4096,256]{1,0:T(8,128)}, u32[]{:S(2)}) copy-start(f32[4096,256]{1,0:T(8,128)} %get-tuple-element.110) | copy-start | bytes 12582916
  88.0 24.8 %collective-permute-start.14 = (f16[4,256,384]{2,1,0:T(8,128)(2,1)S(1)}, f16[4,256,384]{2,1,0:T(8,128)(2,1)S(1)}, u32[]{:S(2)}, u32[]{:S(2)}) collective-permute-start(f16[4,256,384]{2,1,0:T(8,128)(2,1)S(1)} %dynamic-slice_bitcast_fusion), channel_id=1, source_target_pairs={{0,1},{32,33},{64,65},{96,97},{1,0},{33,32},{65,64},{97,96},{2,3},... | collective-permute-start | bytes 2359304 | tf_op jit(solution)/shard_map/ppermute | solution.py:258
  91.2 11.1 %collective-permute-start.10 = (f16[512,384]{1,0:T(8,128)(2,1)S(1)}, f16[512,384]{1,0:T(8,128)(2,1)S(1)}, u32[]{:S(2)}, u32[]{:S(2)}) collective-permute-start(f16[512,384]{1,0:T(8,128)(2,1)S(1)} %get-tuple-element.100), channel_id=1, source_target_pairs={{0,2},{32,34},{64,66},{96,98},{1,3},{33,35},{65,67},{97,99},{2,4},... | collective-permute-start | bytes 1179656 | tf_op jit(solution)/shard_map/ppermute | solution.py:258
  92.7 16.1 %collective-permute-start.20 = (f16[1024,256]{1,0:T(8,128)(2,1)S(1)}, f16[1024,256]{1,0:T(8,128)(2,1)S(1)}, u32[]{:S(2)}, u32[]{:S(2)}) collective-permute-start(f16[1024,256]{1,0:T(8,128)(2,1)S(1)} %pad_maximum_fusion.2), channel_id=1, source_target_pairs={{0,24},{32,56},{64,88},{96,120},{1,25},{33,57},{65,89},{97,121},{2... | collective-permute-start | bytes 1572872 | tf_op jit(solution)/shard_map/ppermute | solution.py:258
  94.8 13.9 %collective-permute-start.17 = (f16[1024,256]{1,0:T(8,128)(2,1)S(1)}, f16[1024,256]{1,0:T(8,128)(2,1)S(1)}, u32[]{:S(2)}, u32[]{:S(2)}) collective-permute-start(f16[1024,256]{1,0:T(8,128)(2,1)S(1)} %pad_maximum_fusion.3), channel_id=1, source_target_pairs={{0,8},{32,40},{64,72},{96,104},{1,9},{33,41},{65,73},{97,105},{2,1... | collective-permute-start | bytes 1572872 | tf_op jit(solution)/shard_map/ppermute | solution.py:258
  94.8 9.8 %collective-permute-start.8 = (f16[512,384]{1,0:T(8,128)(2,1)S(1)}, f16[512,384]{1,0:T(8,128)(2,1)S(1)}, u32[]{:S(2)}, u32[]{:S(2)}) collective-permute-start(f16[512,384]{1,0:T(8,128)(2,1)S(1)} %get-tuple-element.98), channel_id=1, source_target_pairs={{0,6},{32,38},{64,70},{96,102},{1,7},{33,39},{65,71},{97,103},{2,0... | collective-permute-start | bytes 1179656 | tf_op jit(solution)/shard_map/ppermute | solution.py:258
  104.7 7.8 %collective-permute-start.11 = (f16[256,384]{1,0:T(8,128)(2,1)S(1)}, f16[256,384]{1,0:T(8,128)(2,1)S(1)}, u32[]{:S(2)}, u32[]{:S(2)}) collective-permute-start(f16[256,384]{1,0:T(8,128)(2,1)S(1)} %get-tuple-element.101), channel_id=1, source_target_pairs={{0,2},{32,34},{64,66},{96,98},{1,3},{33,35},{65,67},{97,99},{2,4},... | collective-permute-start | bytes 589832 | tf_op jit(solution)/shard_map/ppermute | solution.py:258
  105.8 6.8 %collective-permute-start.12 = (f16[256,384]{1,0:T(8,128)(2,1)S(1)}, f16[256,384]{1,0:T(8,128)(2,1)S(1)}, u32[]{:S(2)}, u32[]{:S(2)}) collective-permute-start(f16[256,384]{1,0:T(8,128)(2,1)S(1)} %get-tuple-element.102), channel_id=1, source_target_pairs={{0,6},{32,38},{64,70},{96,102},{1,7},{33,39},{65,71},{97,103},{2,0... | collective-permute-start | bytes 589832 | tf_op jit(solution)/shard_map/ppermute | solution.py:258
  109.0 7.9 %collective-permute-start.18 = (f16[512,256]{1,0:T(8,128)(2,1)S(1)}, f16[512,256]{1,0:T(8,128)(2,1)S(1)}, u32[]{:S(2)}, u32[]{:S(2)}) collective-permute-start(f16[512,256]{1,0:T(8,128)(2,1)S(1)} %get-tuple-element.117), channel_id=1, source_target_pairs={{0,8},{32,40},{64,72},{96,104},{1,9},{33,41},{65,73},{97,105},{2,1... | collective-permute-start | bytes 786440 | tf_op jit(solution)/shard_map/ppermute | solution.py:258
  109.1 7.8 %collective-permute-start.21 = (f16[512,256]{1,0:T(8,128)(2,1)S(1)}, f16[512,256]{1,0:T(8,128)(2,1)S(1)}, u32[]{:S(2)}, u32[]{:S(2)}) collective-permute-start(f16[512,256]{1,0:T(8,128)(2,1)S(1)} %get-tuple-element.120), channel_id=1, source_target_pairs={{0,24},{32,56},{64,88},{96,120},{1,25},{33,57},{65,89},{97,121},{2... | collective-permute-start | bytes 786440 | tf_op jit(solution)/shard_map/ppermute | solution.py:258
  113.1 8.9 %collective-permute-start.26 = (f32[256,128]{1,0:T(8,128)S(1)}, f32[256,128]{1,0:T(8,128)S(1)}, u32[]{:S(2)}, u32[]{:S(2)}) collective-permute-start(f32[256,128]{1,0:T(8,128)S(1)} %add.303), channel_id=1, source_target_pairs={{0,64},{32,96},{64,0},{96,32},{1,65},{33,97},{65,1},{97,33},{2,66}... | collective-permute-start | bytes 393224 | tf_op jit(solution)/shard_map/ppermute | solution.py:258
  113.9 10.2 %collective-permute-start.15 = (f16[256,384]{1,0:T(8,128)(2,1)S(1)}, f16[256,384]{1,0:T(8,128)(2,1)S(1)}, u32[]{:S(2)}, u32[]{:S(2)}) collective-permute-start(f16[256,384]{1,0:T(8,128)(2,1)S(1)} %fusion.8), channel_id=1, source_target_pairs={{0,1},{32,33},{64,65},{96,97},{1,0},{33,32},{65,64},{97,96},{2,3},... | collective-permute-start | bytes 589832 | tf_op jit(solution)/shard_map/ppermute | solution.py:258
  116.9 10.7 %collective-permute-start.19 = (f16[256,384]{1,0:T(8,128)(2,1)S(1)}, f16[256,384]{1,0:T(8,128)(2,1)S(1)}, u32[]{:S(2)}, u32[]{:S(2)}) collective-permute-start(f16[256,384]{1,0:T(8,128)(2,1)S(1)} %get-tuple-element.118), channel_id=1, source_target_pairs={{0,8},{32,40},{64,72},{96,104},{1,9},{33,41},{65,73},{97,105},{2,1... | collective-permute-start | bytes 589832 | tf_op jit(solution)/shard_map/ppermute | solution.py:258
  116.9 11.3 %collective-permute-start.22 = (f16[256,384]{1,0:T(8,128)(2,1)S(1)}, f16[256,384]{1,0:T(8,128)(2,1)S(1)}, u32[]{:S(2)}, u32[]{:S(2)}) collective-permute-start(f16[256,384]{1,0:T(8,128)(2,1)S(1)} %get-tuple-element.121), channel_id=1, source_target_pairs={{0,24},{32,56},{64,88},{96,120},{1,25},{33,57},{65,89},{97,121},{2... | collective-permute-start | bytes 589832 | tf_op jit(solution)/shard_map/ppermute | solution.py:258
  120.4 1.6 %copy-start.5 = (f32[256,1024]{1,0:T(8,128)S(1)}, f32[256,1024]{1,0:T(8,128)}, u32[]{:S(2)}) copy-start(f32[256,1024]{1,0:T(8,128)} %momentum.1) | copy-start | bytes 3145732
  120.4 7.8 %collective-permute-start.16 = (f16[256,384]{1,0:T(8,128)(2,1)S(1)}, f16[256,384]{1,0:T(8,128)(2,1)S(1)}, u32[]{:S(2)}, u32[]{:S(2)}) collective-permute-start(f16[256,384]{1,0:T(8,128)(2,1)S(1)} %get-tuple-element.149), channel_id=1, source_target_pairs={{0,16},{32,48},{64,80},{96,112},{1,17},{33,49},{65,81},{97,113},{2... | collective-permute-start | bytes 589832 | tf_op jit(solution)/shard_map/ppermute | solution.py:258
  124.1 10.0 %copy-start.3 = (f32[1,256,1024]{2,1,0:T(8,128)S(1)}, f32[1,256,1024]{2,1,0:T(8,128)}, u32[]{:S(2)}) copy-start(f32[1,256,1024]{2,1,0:T(8,128)} %param.11) | copy-start | bytes 3145732
  124.1 10.0 %copy-start.4 = (f32[1,256,1024]{2,1,0:T(8,128)S(1)}, f32[1,256,1024]{2,1,0:T(8,128)}, u32[]{:S(2)}) copy-start(f32[1,256,1024]{2,1,0:T(8,128)} %param.12) | copy-start | bytes 3145732
  124.3 6.2 %collective-permute-start.24 = (f16[256,256]{1,0:T(8,128)(2,1)S(1)}, f16[256,256]{1,0:T(8,128)(2,1)S(1)}, u32[]{:S(2)}, u32[]{:S(2)}) collective-permute-start(f16[256,256]{1,0:T(8,128)(2,1)S(1)} %get-tuple-element.123), channel_id=1, source_target_pairs={{0,2},{32,34},{64,66},{96,98},{1,3},{33,35},{65,67},{97,99},{2,4},... | collective-permute-start | bytes 393224 | tf_op jit(solution)/shard_map/ppermute | solution.py:258
  124.5 7.0 %collective-permute-start.25 = (f16[256,256]{1,0:T(8,128)(2,1)S(1)}, f16[256,256]{1,0:T(8,128)(2,1)S(1)}, u32[]{:S(2)}, u32[]{:S(2)}) collective-permute-start(f16[256,256]{1,0:T(8,128)(2,1)S(1)} %get-tuple-element.124), channel_id=1, source_target_pairs={{0,6},{32,38},{64,70},{96,102},{1,7},{33,39},{65,71},{97,103},{2,0... | collective-permute-start | bytes 393224 | tf_op jit(solution)/shard_map/ppermute | solution.py:258
  127.6 6.5 %collective-permute-start.23 = (f16[256,256]{1,0:T(8,128)(2,1)S(1)}, f16[256,256]{1,0:T(8,128)(2,1)S(1)}, u32[]{:S(2)}, u32[]{:S(2)}) collective-permute-start(f16[256,256]{1,0:T(8,128)(2,1)S(1)} %get-tuple-element.152), channel_id=1, source_target_pairs={{0,4},{32,36},{64,68},{96,100},{1,5},{33,37},{65,69},{97,101},{2,6... | collective-permute-start | bytes 393224 | tf_op jit(solution)/shard_map/ppermute | solution.py:258

commit v2 on v1

--- a/solution.py
+++ b/solution.py
@@ -166,21 +166,23 @@
     )(ids, in_hbm(acts), in_hbm(cots))
 
 
-def pair_kernel(ids, acts, cots, mine, other, held, cots_here, mine_here, sems, own_sems):
+def pair_kernel(ids, acts, cots, mine, other, held, cots_here, here, sems, own_sems):
     count, own = ROWS // PAIR, ids[0]
-    copy = pltpu.make_async_copy(cots.at[:, 2 * WIDE :], cots_here, own_sems.at[count])
+    copy = pltpu.make_async_copy(cots.at[:, 2 * WIDE :], cots_here, own_sems.at[2 * count])
     copy.start()
     back = []
     for i, left in streamed(acts, range(2 * count), held, sems, count):
         if i == 0:
             copy.wait()
         for k in range(2):
-            for to, side in ((mine_here, own), (other, 1 - own)):
+            for to, side in ((0, own), (1, 1 - own)):
                 half = left[:, pl.ds(pl.multiple_of(k * BLOCK + side * 256, 256), 256)]
-                to[i * 512 + k * 256 : i * 512 + (k + 1) * 256] = turned(half, cots_here[...])
+                here[to, i * 512 + k * 256 : i * 512 + (k + 1) * 256] = turned(half, cots_here[...])
         cut = pl.ds(i * 512, 512)
-        back.append(pltpu.make_async_copy(mine_here.at[cut], mine.at[cut], own_sems.at[i]))
-        back[-1].start()
+        for to, whole in ((1, other), (0, mine)):
+            sem = own_sems.at[to * count + i]
+            back.append(pltpu.make_async_copy(here.at[to, cut], whole.at[cut], sem))
+            back[-1].start()
     for copy in back:
         copy.wait()
 
@@ -190,19 +192,19 @@
     return pl.pallas_call(
         pair_kernel,
         in_specs=[SMEM_SPEC, ANY_SPEC, ANY_SPEC],
-        out_specs=[ANY_SPEC, VMEM_SPEC],
+        out_specs=[ANY_SPEC, ANY_SPEC],
         out_shape=[
             pltpu.HBM((ROWS // 2, NARROW), jnp.float32),
-            pltpu.VMEM((ROWS // 2, NARROW), jnp.float32),
+            pltpu.HBM((ROWS // 2, NARROW), jnp.float32),
         ],
         scratch_shapes=[
             pltpu.VMEM((SLOTS, TOK, PAIR), acts.dtype),
             pltpu.VMEM((TOK, NARROW), cots.dtype),
-            pltpu.VMEM((ROWS // 2, NARROW), jnp.float32),
+            pltpu.VMEM((2, ROWS // 2, NARROW), jnp.float32),
             pltpu.SemaphoreType.DMA((SLOTS, 2)),
-            pltpu.SemaphoreType.DMA((1 + count,)),
+            pltpu.SemaphoreType.DMA((1 + 2 * count,)),
         ],
-        compiler_params=pltpu.CompilerParams(vmem_limit_bytes=10 << 20),
+        compiler_params=pltpu.CompilerParams(vmem_limit_bytes=15 << 20),
         cost_estimate=SHORT,
         name="dot_pairs",
     )(ids, in_hbm(acts), in_hbm(cots))
@@ -321,7 +323,7 @@
 
 def inner_step(fragment, grad_a, grad_b, grad_c, weights, first, second, mix):
     rows, cols = weights.shape
-    step = 64
+    step = 128
     block = lambda width: pl.BlockSpec((step, width), lambda i, fragment: (i, 0))
     full, head = block(cols), block(HEAD_DIM)
     return pl.pallas_call(

time: 137 us -> 136 us (level)
  local copies, waits for them, and re-layouts: 6.52 us -> 4.51 us
    unnamed x16 -> x14, local copies, waits for them, and re-layouts: 2.64 us -> 0.63 us
    pallas_call x1, Pallas kernels: 8.63 us -> 10 us  [dot_pairs(): pl.pallas_call(pair_kernel, in_specs=[SMEM_SPEC, ANY_SPEC, ANY_SPEC], out...]
  transfers between devices with their start and end apart: 27 -> 27, of which waited for: 8 -> 8; matrix products, arithmetic and copies ran while one was open for 19% -> 19% of each run, Pallas kernels for 17% -> 18%
where the time goes in v2:
time: 136 us
  starting transfers between devices  44.8 us (33%)
  Pallas kernels  37 us (27%)
  other arithmetic  23.8 us (18%)
  waiting for transfers between devices  23.8 us (18%)
  local copies, waits for them, and re-layouts  4.51 us (3%)
  between operations  1.79 us (1%)
    ppermute x27, starting transfers between devices, send(): got = lax.ppermute(value, AXES, pairs_of(**CHANNELS[step]))  44.8 us
    ppermute x27, waiting for transfers between devices, send(): got = lax.ppermute(value, AXES, pairs_of(**CHANNELS[step]))  23.8 us
    pallas_call x1, Pallas kernels, dot_rest(): pl.pallas_call(rest_kernel, in_specs=[SMEM_SPEC, ANY_SPEC, ANY_SPEC], out...  12 us
    pallas_call x1, Pallas kernels, dot_first(): pl.pallas_call(first_kernel, in_specs=[SMEM_SPEC, ANY_SPEC, ANY_SPEC], ou...  10.8 us
    pallas_call x1, Pallas kernels, dot_pairs(): pl.pallas_call(pair_kernel, in_specs=[SMEM_SPEC, ANY_SPEC, ANY_SPEC], out...  10 us
    convert_element_type x4, other arithmetic, per_device(): term = order.ran(order.after(term).astype(SENT))  5.66 us
    add x4, other arithmetic, near(): order.after(half(own[part]), *others) + wide(half(first[axis + way]))  5.39 us
    slice x6, local copies, waits for them, and re-layouts, low(): return value[:value.shape[0] // 2]  2.96 us
  transfers between devices with their start and end apart: 27, of which 8 were waited for; matrix products, arithmetic and copies ran while one was open for 19% of the time, Pallas kernels for 18%

profile of v2, /device:TPU:0, one launch (start us, length us, event | category | flops | bytes accessed | tf_op | source)
XLA Modules:
  0.0 135.7 jit_solution(4030840709842604308)
XLA Ops:
  0.8 10.8 %dot_first.1 = (f32[2048,384]{1,0:T(8,128)S(1)}, f32[2048,384]{1,0:T(8,128)S(1)}, f32[2048,384]{1,0:T(8,128)S(1)}, f32[2048,384]{1,0:T(8,128)S(1)}) custom-call(s32[16]{0:T(128)S(1)} %stack.135.ids, bf16[768,8192]{1,0:T(8,128)(2,1)} %acts.5, bf16[768,1024]{1,0:T(8,128)(2,1)} %cots.5), custom_call_target="tpu_custom_call" | custom-call | flops 1 | bytes 1 | tf_op jit(solution)/shard_map/dot_first/pallas_call | solution.py:152
  11.6 1.4 %convert_element_type.226 = f16[2048,384]{1,0:T(8,128)(2,1)} convert(f32[2048,384]{1,0:T(8,128)S(1)} %get-tuple-element.72) | non-fusion elementwise | flops 786432 | bytes 4718592 | tf_op jit(solution)/shard_map/convert_element_type | solution.py:378
  13.0 2.0 %collective-permute-start.1 = (f16[2048,384]{1,0:T(8,128)(2,1)}, f16[2048,384]{1,0:T(8,128)(2,1)}, u32[]{:S(2)}, u32[]{:S(2)}) collective-permute-start(f16[2048,384]{1,0:T(8,128)(2,1)} %convert_element_type.226), channel_id=1, source_target_pairs={{0,8},{32,40},{64,72},{96,104},{1,9},{33,41},{65,73},{97,105},{2,1... | collective-permute-start | bytes 4718600 | tf_op jit(solution)/shard_map/ppermute | solution.py:260
  15.0 1.4 %convert_element_type.227 = f16[2048,384]{1,0:T(8,128)(2,1)} convert(f32[2048,384]{1,0:T(8,128)S(1)} %get-tuple-element.73) | non-fusion elementwise | flops 786432 | bytes 4718592 | tf_op jit(solution)/shard_map/convert_element_type | solution.py:378
  16.4 2.1 %collective-permute-start.2 = (f16[2048,384]{1,0:T(8,128)(2,1)}, f16[2048,384]{1,0:T(8,128)(2,1)}, u32[]{:S(2)}, u32[]{:S(2)}) collective-permute-start(f16[2048,384]{1,0:T(8,128)(2,1)} %convert_element_type.227), channel_id=1, source_target_pairs={{0,24},{32,56},{64,88},{96,120},{1,25},{33,57},{65,89},{97,121},{2... | collective-permute-start | bytes 4718600 | tf_op jit(solution)/shard_map/ppermute | solution.py:260
  18.5 1.4 %convert_element_type.228 = f16[2048,384]{1,0:T(8,128)(2,1)} convert(f32[2048,384]{1,0:T(8,128)S(1)} %get-tuple-element.74) | non-fusion elementwise | flops 786432 | bytes 4718592 | tf_op jit(solution)/shard_map/convert_element_type | solution.py:378
  19.9 1.5 %collective-permute-start.3 = (f16[2048,384]{1,0:T(8,128)(2,1)}, f16[2048,384]{1,0:T(8,128)(2,1)}, u32[]{:S(2)}, u32[]{:S(2)}) collective-permute-start(f16[2048,384]{1,0:T(8,128)(2,1)} %convert_element_type.228), channel_id=1, source_target_pairs={{0,2},{32,34},{64,66},{96,98},{1,3},{33,35},{65,67},{97,99},{2,4},... | collective-permute-start | bytes 4718600 | tf_op jit(solution)/shard_map/ppermute | solution.py:260
  21.4 1.4 %convert_element_type.229 = f16[2048,384]{1,0:T(8,128)(2,1)} convert(f32[2048,384]{1,0:T(8,128)S(1)} %get-tuple-element.75) | non-fusion elementwise | flops 786432 | bytes 4718592 | tf_op jit(solution)/shard_map/convert_element_type | solution.py:378
  23.7 2.0 %collective-permute-start.4 = (f16[2048,384]{1,0:T(8,128)(2,1)}, f16[2048,384]{1,0:T(8,128)(2,1)}, u32[]{:S(2)}, u32[]{:S(2)}) collective-permute-start(f16[2048,384]{1,0:T(8,128)(2,1)} %convert_element_type.229), channel_id=1, source_target_pairs={{0,6},{32,38},{64,70},{96,102},{1,7},{33,39},{65,71},{97,103},{2,0... | collective-permute-start | bytes 4718600 | tf_op jit(solution)/shard_map/ppermute | solution.py:260
  25.7 10.0 %dot_pairs.1 = (f32[4096,256]{1,0:T(8,128)}, f32[4096,256]{1,0:T(8,128)}) custom-call(s32[1]{0:T(128)} %bitcast.16.ids, bf16[768,8192]{1,0:T(8,128)(2,1)} %acts.5, bf16[768,1024]{1,0:T(8,128)(2,1)} %cots.5), custom_call_target="tpu_custom_call" | custom-call | flops 1 | bytes 1 | tf_op jit(solution)/shard_map/dot_pairs/pallas_call | solution.py:192
  35.8 2.5 %convert_element_type.230 = f16[4096,256]{1,0:T(8,128)(2,1)S(1)} convert(f32[4096,256]{1,0:T(8,128)} %get-tuple-element.79) | non-fusion elementwise | flops 1048576 | bytes 6291456 | tf_op jit(solution)/shard_map/convert_element_type | solution.py:389
  38.3 3.3 %collective-permute-start.13 = (f16[4096,256]{1,0:T(8,128)(2,1)S(1)}, f16[4096,256]{1,0:T(8,128)(2,1)S(1)}, u32[]{:S(2)}, u32[]{:S(2)}) collective-permute-start(f16[4096,256]{1,0:T(8,128)(2,1)S(1)} %convert_element_type.230), channel_id=1, source_target_pairs={{0,1},{32,33},{64,65},{96,97},{1,0},{33,32},{65,64},{97,96},{2,3},... | collective-permute-start | bytes 6291464 | tf_op jit(solution)/shard_map/ppermute | solution.py:260
  41.6 12.0 %dot_rest.1 = (f32[1024,384]{1,0:T(8,128)S(1)}, f32[1024,384]{1,0:T(8,128)S(1)}, f32[1024,384]{1,0:T(8,128)S(1)}, f32[1024,384]{1,0:T(8,128)S(1)}, f32[2048,384]{1,0:T(8,128)}, /*index=5*/f32[2048,384]{1,0:T(8,128)}) custom-call(s32[16]{0:T(128)S(1)} %stack.118.ids, bf16[768,8192]{1,0:T(8,128)(2,1)} %acts.5, bf16[768,1024]{1,0:T(8,128)(2,1)} %cots.5), custom_call_target="tpu_custom_call" | custom-call | flops 1 | bytes 1 | tf_op jit(solution)/shard_map/dot_rest/pallas_call | solution.py:114
  53.6 2.2 %fusion.10 = (f32[1024,384]{1,0:T(8,128)S(1)}, f32[1024,384]{1,0:T(8,128)S(1)}) fusion(f32[2048,384]{1,0:T(8,128)} %get-tuple-element.81), kind=kLoop, calls=%fused_computation.69 | loop fusion | bytes 6291456 | tf_op jit(solution)/shard_map/slice | solution.py:345
  55.8 0.6 copy-done.6
  56.6 1.4 %add_convert_fusion.8 = f16[1024,384]{1,0:T(8,128)(2,1)S(1)} fusion(f32[1024,384]{1,0:T(8,128)S(1)} %get-tuple-element.85, f16[2048,384]{1,0:T(8,128)(2,1)} %collective-permute-done.1), kind=kLoop, calls=%fused_computation.16 | loop fusion | flops 1179648 | bytes 3145728 | tf_op jit(solution)/shard_map/convert_element_type | solution.py:411
  58.3 1.4 %add_convert_fusion.7 = f16[1024,384]{1,0:T(8,128)(2,1)S(1)} fusion(f32[1024,384]{1,0:T(8,128)S(1)} %get-tuple-element.86, f16[2048,384]{1,0:T(8,128)(2,1)} %collective-permute-done.2), kind=kLoop, calls=%fused_computation.15 | loop fusion | flops 1179648 | bytes 3145728 | tf_op jit(solution)/shard_map/convert_element_type | solution.py:413
  59.7 3.3 %collective-permute-start.6 = (f16[1024,384]{1,0:T(8,128)(2,1)S(1)}, f16[1024,384]{1,0:T(8,128)(2,1)S(1)}, u32[]{:S(2)}, u32[]{:S(2)}) collective-permute-start(f16[1024,384]{1,0:T(8,128)(2,1)S(1)} %add_convert_fusion.7), channel_id=1, source_target_pairs={{0,24},{32,56},{64,88},{96,120},{1,25},{33,57},{65,89},{97,121},{2... | collective-permute-start | bytes 2359304 | tf_op jit(solution)/shard_map/ppermute | solution.py:260
  63.0 1.4 %add_convert_fusion.6 = f16[1024,384]{1,0:T(8,128)(2,1)S(1)} fusion(f32[1024,384]{1,0:T(8,128)S(1)} %get-tuple-element.87, f16[2048,384]{1,0:T(8,128)(2,1)} %collective-permute-done.3), kind=kLoop, calls=%fused_computation.14 | loop fusion | flops 1179648 | bytes 3145728 | tf_op jit(solution)/shard_map/convert_element_type | solution.py:411
  64.7 1.4 %add_convert_fusion.5 = f16[1024,384]{1,0:T(8,128)(2,1)S(1)} fusion(f32[1024,384]{1,0:T(8,128)S(1)} %get-tuple-element.88, f16[2048,384]{1,0:T(8,128)(2,1)} %collective-permute-done.4), kind=kLoop, calls=%fused_computation.13 | loop fusion | flops 1179648 | bytes 3145728 | tf_op jit(solution)/shard_map/convert_element_type | solution.py:413
  66.1 3.0 %collective-permute-start.7 = (f16[1024,384]{1,0:T(8,128)(2,1)S(1)}, f16[1024,384]{1,0:T(8,128)(2,1)S(1)}, u32[]{:S(2)}, u32[]{:S(2)}) collective-permute-start(f16[1024,384]{1,0:T(8,128)(2,1)S(1)} %add_convert_fusion.5), channel_id=1, source_target_pairs={{0,6},{32,38},{64,70},{96,102},{1,7},{33,39},{65,71},{97,103},{2,0... | collective-permute-start | bytes 2359304 | tf_op jit(solution)/shard_map/ppermute | solution.py:260
  69.1 9.5 %collective-permute-done.5 = f16[1024,384]{1,0:T(8,128)(2,1)S(1)} collective-permute-done((f16[1024,384]{1,0:T(8,128)(2,1)S(1)}, f16[1024,384]{1,0:T(8,128)(2,1)S(1)}, u32[]{:S(2)}, u32[]{:S(2)}) %collective-permute-start.5) | collective-permute-done | bytes 786464 | tf_op jit(solution)/shard_map/ppermute | solution.py:260
  78.6 1.4 %convert_add_fusion.4 = f32[1024,384]{1,0:T(8,128)S(1)} fusion(f32[1024,384]{1,0:T(8,128)S(1)} %get-tuple-element.90, f16[2048,384]{1,0:T(8,128)(2,1)} %collective-permute-done.2), kind=kLoop, calls=%fused_computation.12 | loop fusion | flops 786432 | bytes 3932160 | tf_op jit(solution)/shard_map/add | solution.py:404
  80.0 1.4 %convert_add_fusion.3 = f32[1024,384]{1,0:T(8,128)S(1)} fusion(f32[1024,384]{1,0:T(8,128)S(1)} %get-tuple-element.91, f16[2048,384]{1,0:T(8,128)(2,1)} %collective-permute-done.1), kind=kLoop, calls=%fused_computation.11 | loop fusion | flops 786432 | bytes 3932160 | tf_op jit(solution)/shard_map/add | solution.py:404
  82.7 1.3 convert_add_fusion.2
  84.0 1.4 %convert_add_fusion.1 = f32[1024,384]{1,0:T(8,128)S(1)} fusion(f32[1024,384]{1,0:T(8,128)S(1)} %get-tuple-element.106, f16[2048,384]{1,0:T(8,128)(2,1)} %collective-permute-done.3), kind=kLoop, calls=%fused_computation.7 | loop fusion | flops 786432 | bytes 3932160 | tf_op jit(solution)/shard_map/add | solution.py:404
  86.5 0.9 collective-permute-done.13
  87.4 3.2 %collective-permute-start.14 = (f16[4,256,384]{2,1,0:T(8,128)(2,1)S(1)}, f16[4,256,384]{2,1,0:T(8,128)(2,1)S(1)}, u32[]{:S(2)}, u32[]{:S(2)}) collective-permute-start(f16[4,256,384]{2,1,0:T(8,128)(2,1)S(1)} %dynamic-slice_bitcast_fusion), channel_id=1, source_target_pairs={{0,1},{32,33},{64,65},{96,97},{1,0},{33,32},{65,64},{97,96},{2,3},... | collective-permute-start | bytes 2359304 | tf_op jit(solution)/shard_map/ppermute | solution.py:260
  90.9 0.7 add_convert_fusion
  92.1 2.1 %collective-permute-start.20 = (f16[1024,256]{1,0:T(8,128)(2,1)S(1)}, f16[1024,256]{1,0:T(8,128)(2,1)S(1)}, u32[]{:S(2)}, u32[]{:S(2)}) collective-permute-start(f16[1024,256]{1,0:T(8,128)(2,1)S(1)} %pad_maximum_fusion.2), channel_id=1, source_target_pairs={{0,24},{32,56},{64,88},{96,120},{1,25},{33,57},{65,89},{97,121},{2... | collective-permute-start | bytes 1572872 | tf_op jit(solution)/shard_map/ppermute | solution.py:260
  94.2 2.9 %collective-permute-start.8 = (f16[512,384]{1,0:T(8,128)(2,1)S(1)}, f16[512,384]{1,0:T(8,128)(2,1)S(1)}, u32[]{:S(2)}, u32[]{:S(2)}) collective-permute-start(f16[512,384]{1,0:T(8,128)(2,1)S(1)} %get-tuple-element.98), channel_id=1, source_target_pairs={{0,6},{32,38},{64,70},{96,102},{1,7},{33,39},{65,71},{97,103},{2,0... | collective-permute-start | bytes 1179656 | tf_op jit(solution)/shard_map/ppermute | solution.py:260
  97.3 4.3 %collective-permute-done.10 = f16[512,384]{1,0:T(8,128)(2,1)S(1)} collective-permute-done((f16[512,384]{1,0:T(8,128)(2,1)S(1)}, f16[512,384]{1,0:T(8,128)(2,1)S(1)}, u32[]{:S(2)}, u32[]{:S(2)}) %collective-permute-start.10) | collective-permute-done | bytes 393248 | tf_op jit(solution)/shard_map/ppermute | solution.py:260
  101.7 2.2 %collective-permute-done.8 = f16[512,384]{1,0:T(8,128)(2,1)S(1)} collective-permute-done((f16[512,384]{1,0:T(8,128)(2,1)S(1)}, f16[512,384]{1,0:T(8,128)(2,1)S(1)}, u32[]{:S(2)}, u32[]{:S(2)}) %collective-permute-start.8) | collective-permute-done | bytes 393248 | tf_op jit(solution)/shard_map/ppermute | solution.py:260
  104.1 1.1 collective-permute-start.11
  105.2 2.8 %collective-permute-start.12 = (f16[256,384]{1,0:T(8,128)(2,1)S(1)}, f16[256,384]{1,0:T(8,128)(2,1)S(1)}, u32[]{:S(2)}, u32[]{:S(2)}) collective-permute-start(f16[256,384]{1,0:T(8,128)(2,1)S(1)} %get-tuple-element.102), channel_id=1, source_target_pairs={{0,6},{32,38},{64,70},{96,102},{1,7},{33,39},{65,71},{97,103},{2,0... | collective-permute-start | bytes 589832 | tf_op jit(solution)/shard_map/ppermute | solution.py:260
  108.5 3.2 %collective-permute-start.21 = (f16[512,256]{1,0:T(8,128)(2,1)S(1)}, f16[512,256]{1,0:T(8,128)(2,1)S(1)}, u32[]{:S(2)}, u32[]{:S(2)}) collective-permute-start(f16[512,256]{1,0:T(8,128)(2,1)S(1)} %get-tuple-element.120), channel_id=1, source_target_pairs={{0,24},{32,56},{64,88},{96,120},{1,25},{33,57},{65,89},{97,121},{2... | collective-permute-start | bytes 786440 | tf_op jit(solution)/shard_map/ppermute | solution.py:260
  112.5 0.8 collective-permute-start.26
  113.3 1.8 %collective-permute-start.15 = (f16[256,384]{1,0:T(8,128)(2,1)S(1)}, f16[256,384]{1,0:T(8,128)(2,1)S(1)}, u32[]{:S(2)}, u32[]{:S(2)}) collective-permute-start(f16[256,384]{1,0:T(8,128)(2,1)S(1)} %fusion.8), channel_id=1, source_target_pairs={{0,1},{32,33},{64,65},{96,97},{1,0},{33,32},{65,64},{97,96},{2,3},... | collective-permute-start | bytes 589832 | tf_op jit(solution)/shard_map/ppermute | solution.py:260
  115.2 1.1 collective-permute-done.18
  116.3 3.5 %collective-permute-start.22 = (f16[256,384]{1,0:T(8,128)(2,1)S(1)}, f16[256,384]{1,0:T(8,128)(2,1)S(1)}, u32[]{:S(2)}, u32[]{:S(2)}) collective-permute-start(f16[256,384]{1,0:T(8,128)(2,1)S(1)} %get-tuple-element.121), channel_id=1, source_target_pairs={{0,24},{32,56},{64,88},{96,120},{1,25},{33,57},{65,89},{97,121},{2... | collective-permute-start | bytes 589832 | tf_op jit(solution)/shard_map/ppermute | solution.py:260
  119.8 1.2 collective-permute-start.16
  121.4 2.0 %outer_step.1 = (f32[256,1024]{1,0:T(8,128)}, f32[256,1024]{1,0:T(8,128)}, f32[256,128]{1,0:T(8,128)S(1)}) custom-call(s32[1]{0:T(128)S(6)} %copy.15.fragment, f32[256,1024]{1,0:T(8,128)S(1)} %copy-done.1, f32[256,1024]{1,0:T(8,128)S(1)} %copy-done.4, f32[256,128]{1,0:T(8,128)S(1)} %add_multiply_fusion.drift), custom_call_target="tpu_custom_call" | custom-call | flops 1 | bytes 1 | tf_op jit(solution)/shard_map/outer_step/pallas_call | solution.py:285
  123.9 3.1 %collective-permute-start.25 = (f16[256,256]{1,0:T(8,128)(2,1)S(1)}, f16[256,256]{1,0:T(8,128)(2,1)S(1)}, u32[]{:S(2)}, u32[]{:S(2)}) collective-permute-start(f16[256,256]{1,0:T(8,128)(2,1)S(1)} %get-tuple-element.124), channel_id=1, source_target_pairs={{0,6},{32,38},{64,70},{96,102},{1,7},{33,39},{65,71},{97,103},{2,0... | collective-permute-start | bytes 393224 | tf_op jit(solution)/shard_map/ppermute | solution.py:260
  127.0 0.6 collective-permute-start.23
  127.7 2.2 %collective-permute-done.24 = f16[256,256]{1,0:T(8,128)(2,1)S(1)} collective-permute-done((f16[256,256]{1,0:T(8,128)(2,1)S(1)}, f16[256,256]{1,0:T(8,128)(2,1)S(1)}, u32[]{:S(2)}, u32[]{:S(2)}) %collective-permute-start.24) | collective-permute-done | bytes 131104 | tf_op jit(solution)/shard_map/ppermute | solution.py:260
  129.9 1.0 collective-permute-done.25
  130.9 2.6 %collective-permute-done.23 = f16[256,256]{1,0:T(8,128)(2,1)S(1)} collective-permute-done((f16[256,256]{1,0:T(8,128)(2,1)S(1)}, f16[256,256]{1,0:T(8,128)(2,1)S(1)}, u32[]{:S(2)}, u32[]{:S(2)}) %collective-permute-start.23) | collective-permute-done | bytes 131104 | tf_op jit(solution)/shard_map/ppermute | solution.py:260
  133.5 2.2 %inner_step.1 = (f32[256,1024]{1,0:T(8,128)}, f32[256,1024]{1,0:T(8,128)}, f32[256,1024]{1,0:T(8,128)}) custom-call(s32[1]{0:T(128)S(6)} %copy.15.fragment, f32[256,384]{1,0:T(8,128)S(1)} %bitcast_add_fusion.grad_a, f32[256,384]{1,0:T(8,128)S(1)} %fusion.4.grad_b, f32[256,256]{1,0:T(8,128)S(1)} %fusion.7.grad_c, f32[256,1024]{1,0:T(8,128)S(1)} %bitcast.122, ...), custom_call_target="tpu_custom_call" | custom-call | flops 1 | bytes 1 | tf_op jit(solution)/shard_map/inner_step/pallas_call | solution.py:329
  (79 shorter events, 7.1 us)
Async XLA Ops:
  13.0 43.6 %collective-permute-start.1 = (f16[2048,384]{1,0:T(8,128)(2,1)}, f16[2048,384]{1,0:T(8,128)(2,1)}, u32[]{:S(2)}, u32[]{:S(2)}) collective-permute-start(f16[2048,384]{1,0:T(8,128)(2,1)} %convert_element_type.226), channel_id=1, source_target_pairs={{0,8},{32,40},{64,72},{96,104},{1,9},{33,41},{65,73},{97,105},{2,1... | collective-permute-start | bytes 4718600 | tf_op jit(solution)/shard_map/ppermute | solution.py:260
  16.4 41.9 %collective-permute-start.2 = (f16[2048,384]{1,0:T(8,128)(2,1)}, f16[2048,384]{1,0:T(8,128)(2,1)}, u32[]{:S(2)}, u32[]{:S(2)}) collective-permute-start(f16[2048,384]{1,0:T(8,128)(2,1)} %convert_element_type.227), channel_id=1, source_target_pairs={{0,24},{32,56},{64,88},{96,120},{1,25},{33,57},{65,89},{97,121},{2... | collective-permute-start | bytes 4718600 | tf_op jit(solution)/shard_map/ppermute | solution.py:260
  19.9 43.1 %collective-permute-start.3 = (f16[2048,384]{1,0:T(8,128)(2,1)}, f16[2048,384]{1,0:T(8,128)(2,1)}, u32[]{:S(2)}, u32[]{:S(2)}) collective-permute-start(f16[2048,384]{1,0:T(8,128)(2,1)} %convert_element_type.228), channel_id=1, source_target_pairs={{0,2},{32,34},{64,66},{96,98},{1,3},{33,35},{65,67},{97,99},{2,4},... | collective-permute-start | bytes 4718600 | tf_op jit(solution)/shard_map/ppermute | solution.py:260
  21.4 2.1 %copy-start = (f32[1,256,1024]{2,1,0:T(8,128)S(1)}, f32[1,256,1024]{2,1,0:T(8,128)}, u32[]{:S(2)}) copy-start(f32[1,256,1024]{2,1,0:T(8,128)} %param.10) | copy-start | bytes 3145732
  21.4 2.1 %copy-start.1 = (f32[256,1024]{1,0:T(8,128)S(1)}, f32[256,1024]{1,0:T(8,128)}, u32[]{:S(2)}) copy-start(f32[256,1024]{1,0:T(8,128)} %anchor.1) | copy-start | bytes 3145732
  23.6 12.2 %collective-permute-start = (f32[256,128]{1,0:T(8,128)S(1)}, f32[256,128]{1,0:T(8,128)S(1)}, u32[]{:S(2)}, u32[]{:S(2)}) collective-permute-start(f32[256,128]{1,0:T(8,128)S(1)} %bitcast_subtract_fusion), channel_id=1, source_target_pairs={{0,32},{32,0},{64,96},{96,64},{1,33},{33,1},{65,97},{97,65},{2,34}... | collective-permute-start | bytes 393224 | tf_op jit(solution)/shard_map/ppermute | solution.py:260
  23.7 41.1 %collective-permute-start.4 = (f16[2048,384]{1,0:T(8,128)(2,1)}, f16[2048,384]{1,0:T(8,128)(2,1)}, u32[]{:S(2)}, u32[]{:S(2)}) collective-permute-start(f16[2048,384]{1,0:T(8,128)(2,1)} %convert_element_type.229), channel_id=1, source_target_pairs={{0,6},{32,38},{64,70},{96,102},{1,7},{33,39},{65,71},{97,103},{2,0... | collective-permute-start | bytes 4718600 | tf_op jit(solution)/shard_map/ppermute | solution.py:260
  38.3 49.1 %collective-permute-start.13 = (f16[4096,256]{1,0:T(8,128)(2,1)S(1)}, f16[4096,256]{1,0:T(8,128)(2,1)S(1)}, u32[]{:S(2)}, u32[]{:S(2)}) collective-permute-start(f16[4096,256]{1,0:T(8,128)(2,1)S(1)} %convert_element_type.230), channel_id=1, source_target_pairs={{0,1},{32,33},{64,65},{96,97},{1,0},{33,32},{65,64},{97,96},{2,3},... | collective-permute-start | bytes 6291464 | tf_op jit(solution)/shard_map/ppermute | solution.py:260
  53.5 2.8 %copy-start.6 = (f32[2048,384]{1,0:T(8,128)S(1)}, f32[2048,384]{1,0:T(8,128)}, u32[]{:S(2)}) copy-start(f32[2048,384]{1,0:T(8,128)} %get-tuple-element.104) | copy-start | bytes 9437188
  58.0 20.6 %collective-permute-start.5 = (f16[1024,384]{1,0:T(8,128)(2,1)S(1)}, f16[1024,384]{1,0:T(8,128)(2,1)S(1)}, u32[]{:S(2)}, u32[]{:S(2)}) collective-permute-start(f16[1024,384]{1,0:T(8,128)(2,1)S(1)} %add_convert_fusion.8), channel_id=1, source_target_pairs={{0,8},{32,40},{64,72},{96,104},{1,9},{33,41},{65,73},{97,105},{2,1... | collective-permute-start | bytes 2359304 | tf_op jit(solution)/shard_map/ppermute | solution.py:260
  59.7 21.9 %collective-permute-start.6 = (f16[1024,384]{1,0:T(8,128)(2,1)S(1)}, f16[1024,384]{1,0:T(8,128)(2,1)S(1)}, u32[]{:S(2)}, u32[]{:S(2)}) collective-permute-start(f16[1024,384]{1,0:T(8,128)(2,1)S(1)} %add_convert_fusion.7), channel_id=1, source_target_pairs={{0,24},{32,56},{64,88},{96,120},{1,25},{33,57},{65,89},{97,121},{2... | collective-permute-start | bytes 2359304 | tf_op jit(solution)/shard_map/ppermute | solution.py:260
  64.4 21.0 %collective-permute-start.9 = (f16[1024,384]{1,0:T(8,128)(2,1)S(1)}, f16[1024,384]{1,0:T(8,128)(2,1)S(1)}, u32[]{:S(2)}, u32[]{:S(2)}) collective-permute-start(f16[1024,384]{1,0:T(8,128)(2,1)S(1)} %add_convert_fusion.6), channel_id=1, source_target_pairs={{0,2},{32,34},{64,66},{96,98},{1,3},{33,35},{65,67},{97,99},{2,4},... | collective-permute-start | bytes 2359304 | tf_op jit(solution)/shard_map/ppermute | solution.py:260
  66.1 19.5 %collective-permute-start.7 = (f16[1024,384]{1,0:T(8,128)(2,1)S(1)}, f16[1024,384]{1,0:T(8,128)(2,1)S(1)}, u32[]{:S(2)}, u32[]{:S(2)}) collective-permute-start(f16[1024,384]{1,0:T(8,128)(2,1)S(1)} %add_convert_fusion.5), channel_id=1, source_target_pairs={{0,6},{32,38},{64,70},{96,102},{1,7},{33,39},{65,71},{97,103},{2,0... | collective-permute-start | bytes 2359304 | tf_op jit(solution)/shard_map/ppermute | solution.py:260
  85.9 5.0 %copy-start.5 = (f32[4096,256]{1,0:T(8,128)S(1)}, f32[4096,256]{1,0:T(8,128)}, u32[]{:S(2)}) copy-start(f32[4096,256]{1,0:T(8,128)} %get-tuple-element.110) | copy-start | bytes 12582916
  87.4 24.8 %collective-permute-start.14 = (f16[4,256,384]{2,1,0:T(8,128)(2,1)S(1)}, f16[4,256,384]{2,1,0:T(8,128)(2,1)S(1)}, u32[]{:S(2)}, u32[]{:S(2)}) collective-permute-start(f16[4,256,384]{2,1,0:T(8,128)(2,1)S(1)} %dynamic-slice_bitcast_fusion), channel_id=1, source_target_pairs={{0,1},{32,33},{64,65},{96,97},{1,0},{33,32},{65,64},{97,96},{2,3},... | collective-permute-start | bytes 2359304 | tf_op jit(solution)/shard_map/ppermute | solution.py:260
  90.6 11.1 %collective-permute-start.10 = (f16[512,384]{1,0:T(8,128)(2,1)S(1)}, f16[512,384]{1,0:T(8,128)(2,1)S(1)}, u32[]{:S(2)}, u32[]{:S(2)}) collective-permute-start(f16[512,384]{1,0:T(8,128)(2,1)S(1)} %get-tuple-element.100), channel_id=1, source_target_pairs={{0,2},{32,34},{64,66},{96,98},{1,3},{33,35},{65,67},{97,99},{2,4},... | collective-permute-start | bytes 1179656 | tf_op jit(solution)/shard_map/ppermute | solution.py:260
  92.1 16.1 %collective-permute-start.20 = (f16[1024,256]{1,0:T(8,128)(2,1)S(1)}, f16[1024,256]{1,0:T(8,128)(2,1)S(1)}, u32[]{:S(2)}, u32[]{:S(2)}) collective-permute-start(f16[1024,256]{1,0:T(8,128)(2,1)S(1)} %pad_maximum_fusion.2), channel_id=1, source_target_pairs={{0,24},{32,56},{64,88},{96,120},{1,25},{33,57},{65,89},{97,121},{2... | collective-permute-start | bytes 1572872 | tf_op jit(solution)/shard_map/ppermute | solution.py:260
  94.2 13.9 %collective-permute-start.17 = (f16[1024,256]{1,0:T(8,128)(2,1)S(1)}, f16[1024,256]{1,0:T(8,128)(2,1)S(1)}, u32[]{:S(2)}, u32[]{:S(2)}) collective-permute-start(f16[1024,256]{1,0:T(8,128)(2,1)S(1)} %pad_maximum_fusion.3), channel_id=1, source_target_pairs={{0,8},{32,40},{64,72},{96,104},{1,9},{33,41},{65,73},{97,105},{2,1... | collective-permute-start | bytes 1572872 | tf_op jit(solution)/shard_map/ppermute | solution.py:260
  94.2 9.8 %collective-permute-start.8 = (f16[512,384]{1,0:T(8,128)(2,1)S(1)}, f16[512,384]{1,0:T(8,128)(2,1)S(1)}, u32[]{:S(2)}, u32[]{:S(2)}) collective-permute-start(f16[512,384]{1,0:T(8,128)(2,1)S(1)} %get-tuple-element.98), channel_id=1, source_target_pairs={{0,6},{32,38},{64,70},{96,102},{1,7},{33,39},{65,71},{97,103},{2,0... | collective-permute-start | bytes 1179656 | tf_op jit(solution)/shard_map/ppermute | solution.py:260
  104.1 7.8 %collective-permute-start.11 = (f16[256,384]{1,0:T(8,128)(2,1)S(1)}, f16[256,384]{1,0:T(8,128)(2,1)S(1)}, u32[]{:S(2)}, u32[]{:S(2)}) collective-permute-start(f16[256,384]{1,0:T(8,128)(2,1)S(1)} %get-tuple-element.101), channel_id=1, source_target_pairs={{0,2},{32,34},{64,66},{96,98},{1,3},{33,35},{65,67},{97,99},{2,4},... | collective-permute-start | bytes 589832 | tf_op jit(solution)/shard_map/ppermute | solution.py:260
  105.2 6.8 %collective-permute-start.12 = (f16[256,384]{1,0:T(8,128)(2,1)S(1)}, f16[256,384]{1,0:T(8,128)(2,1)S(1)}, u32[]{:S(2)}, u32[]{:S(2)}) collective-permute-start(f16[256,384]{1,0:T(8,128)(2,1)S(1)} %get-tuple-element.102), channel_id=1, source_target_pairs={{0,6},{32,38},{64,70},{96,102},{1,7},{33,39},{65,71},{97,103},{2,0... | collective-permute-start | bytes 589832 | tf_op jit(solution)/shard_map/ppermute | solution.py:260
  108.4 7.9 %collective-permute-start.18 = (f16[512,256]{1,0:T(8,128)(2,1)S(1)}, f16[512,256]{1,0:T(8,128)(2,1)S(1)}, u32[]{:S(2)}, u32[]{:S(2)}) collective-permute-start(f16[512,256]{1,0:T(8,128)(2,1)S(1)} %get-tuple-element.117), channel_id=1, source_target_pairs={{0,8},{32,40},{64,72},{96,104},{1,9},{33,41},{65,73},{97,105},{2,1... | collective-permute-start | bytes 786440 | tf_op jit(solution)/shard_map/ppermute | solution.py:260
  108.5 7.8 %collective-permute-start.21 = (f16[512,256]{1,0:T(8,128)(2,1)S(1)}, f16[512,256]{1,0:T(8,128)(2,1)S(1)}, u32[]{:S(2)}, u32[]{:S(2)}) collective-permute-start(f16[512,256]{1,0:T(8,128)(2,1)S(1)} %get-tuple-element.120), channel_id=1, source_target_pairs={{0,24},{32,56},{64,88},{96,120},{1,25},{33,57},{65,89},{97,121},{2... | collective-permute-start | bytes 786440 | tf_op jit(solution)/shard_map/ppermute | solution.py:260
  112.5 8.9 %collective-permute-start.26 = (f32[256,128]{1,0:T(8,128)S(1)}, f32[256,128]{1,0:T(8,128)S(1)}, u32[]{:S(2)}, u32[]{:S(2)}) collective-permute-start(f32[256,128]{1,0:T(8,128)S(1)} %add.303), channel_id=1, source_target_pairs={{0,64},{32,96},{64,0},{96,32},{1,65},{33,97},{65,1},{97,33},{2,66}... | collective-permute-start | bytes 393224 | tf_op jit(solution)/shard_map/ppermute | solution.py:260
  113.3 10.2 %collective-permute-start.15 = (f16[256,384]{1,0:T(8,128)(2,1)S(1)}, f16[256,384]{1,0:T(8,128)(2,1)S(1)}, u32[]{:S(2)}, u32[]{:S(2)}) collective-permute-start(f16[256,384]{1,0:T(8,128)(2,1)S(1)} %fusion.8), channel_id=1, source_target_pairs={{0,1},{32,33},{64,65},{96,97},{1,0},{33,32},{65,64},{97,96},{2,3},... | collective-permute-start | bytes 589832 | tf_op jit(solution)/shard_map/ppermute | solution.py:260
  116.3 10.7 %collective-permute-start.19 = (f16[256,384]{1,0:T(8,128)(2,1)S(1)}, f16[256,384]{1,0:T(8,128)(2,1)S(1)}, u32[]{:S(2)}, u32[]{:S(2)}) collective-permute-start(f16[256,384]{1,0:T(8,128)(2,1)S(1)} %get-tuple-element.118), channel_id=1, source_target_pairs={{0,8},{32,40},{64,72},{96,104},{1,9},{33,41},{65,73},{97,105},{2,1... | collective-permute-start | bytes 589832 | tf_op jit(solution)/shard_map/ppermute | solution.py:260
  116.3 11.3 %collective-permute-start.22 = (f16[256,384]{1,0:T(8,128)(2,1)S(1)}, f16[256,384]{1,0:T(8,128)(2,1)S(1)}, u32[]{:S(2)}, u32[]{:S(2)}) collective-permute-start(f16[256,384]{1,0:T(8,128)(2,1)S(1)} %get-tuple-element.121), channel_id=1, source_target_pairs={{0,24},{32,56},{64,88},{96,120},{1,25},{33,57},{65,89},{97,121},{2... | collective-permute-start | bytes 589832 | tf_op jit(solution)/shard_map/ppermute | solution.py:260
  119.8 1.6 %copy-start.4 = (f32[256,1024]{1,0:T(8,128)S(1)}, f32[256,1024]{1,0:T(8,128)}, u32[]{:S(2)}) copy-start(f32[256,1024]{1,0:T(8,128)} %momentum.1) | copy-start | bytes 3145732
  119.8 7.8 %collective-permute-start.16 = (f16[256,384]{1,0:T(8,128)(2,1)S(1)}, f16[256,384]{1,0:T(8,128)(2,1)S(1)}, u32[]{:S(2)}, u32[]{:S(2)}) collective-permute-start(f16[256,384]{1,0:T(8,128)(2,1)S(1)} %get-tuple-element.149), channel_id=1, source_target_pairs={{0,16},{32,48},{64,80},{96,112},{1,17},{33,49},{65,81},{97,113},{2... | collective-permute-start | bytes 589832 | tf_op jit(solution)/shard_map/ppermute | solution.py:260
  123.5 10.0 %copy-start.2 = (f32[1,256,1024]{2,1,0:T(8,128)S(1)}, f32[1,256,1024]{2,1,0:T(8,128)}, u32[]{:S(2)}) copy-start(f32[1,256,1024]{2,1,0:T(8,128)} %param.11) | copy-start | bytes 3145732
  123.5 10.0 %copy-start.3 = (f32[1,256,1024]{2,1,0:T(8,128)S(1)}, f32[1,256,1024]{2,1,0:T(8,128)}, u32[]{:S(2)}) copy-start(f32[1,256,1024]{2,1,0:T(8,128)} %param.12) | copy-start | bytes 3145732
  123.7 6.2 %collective-permute-start.24 = (f16[256,256]{1,0:T(8,128)(2,1)S(1)}, f16[256,256]{1,0:T(8,128)(2,1)S(1)}, u32[]{:S(2)}, u32[]{:S(2)}) collective-permute-start(f16[256,256]{1,0:T(8,128)(2,1)S(1)} %get-tuple-element.123), channel_id=1, source_target_pairs={{0,2},{32,34},{64,66},{96,98},{1,3},{33,35},{65,67},{97,99},{2,4},... | collective-permute-start | bytes 393224 | tf_op jit(solution)/shard_map/ppermute | solution.py:260
  123.9 7.0 %collective-permute-start.25 = (f16[256,256]{1,0:T(8,128)(2,1)S(1)}, f16[256,256]{1,0:T(8,128)(2,1)S(1)}, u32[]{:S(2)}, u32[]{:S(2)}) collective-permute-start(f16[256,256]{1,0:T(8,128)(2,1)S(1)} %get-tuple-element.124), channel_id=1, source_target_pairs={{0,6},{32,38},{64,70},{96,102},{1,7},{33,39},{65,71},{97,103},{2,0... | collective-permute-start | bytes 393224 | tf_op jit(solution)/shard_map/ppermute | solution.py:260
  127.0 6.5 %collective-permute-start.23 = (f16[256,256]{1,0:T(8,128)(2,1)S(1)}, f16[256,256]{1,0:T(8,128)(2,1)S(1)}, u32[]{:S(2)}, u32[]{:S(2)}) collective-permute-start(f16[256,256]{1,0:T(8,128)(2,1)S(1)} %get-tuple-element.152), channel_id=1, source_target_pairs={{0,4},{32,36},{64,68},{96,100},{1,5},{33,37},{65,69},{97,101},{2,6... | collective-permute-start | bytes 393224 | tf_op jit(solution)/shard_map/ppermute | solution.py:260
